TPU v7x, 256 devices: a whole 4x4x8 slice. The times are simulated.
256 devices in a mesh: grp: 32 (over x_hi, z, core), blk: 8 (over y, x_lo).
Axes of the slice: x: 4 (x_hi: 2, x_lo: 2; x = x_hi * 2 + x_lo), y: 4, z: 8, core: 2. Of those that a mesh axis runs over, the one named last changes fastest.
Arguments:
- q_latent: bfloat16 [256, 2, 64, 512], P(('grp', 'blk')), may hold values from -13 to 13
- q_rope: bfloat16 [256, 2, 4096], P(('grp', 'blk')), may hold values from -6 to 6
- prefix_latent: bfloat16 [32, 16384, 512], P('grp', 'blk'), may hold values from -6 to 6
- prefix_rope: bfloat16 [32, 64, 16384], P('grp', None, 'blk'), may hold values from -6 to 6
- suffix_latent: bfloat16 [256, 2048, 512], P(('grp', 'blk')), may hold values from -6 to 6
- suffix_rope: bfloat16 [256, 64, 2048], P(('grp', 'blk')), may hold values from -6 to 6
- prefix_of: int32 [8, 32, 1], P('blk'), may hold values from 0 to 31; in each aligned block of 32 rows (0 to 31, 32 to 63, ..., all dimensions but the last counted through in order) at most 2 rows name the same one
- suffix_len: int32 [256], P(('grp', 'blk')), may hold values from 1 to 2046, 261888 in all
Outputs:
- attended: bfloat16 [256, 2, 64, 512], P(('grp', 'blk'))
Inputs may be any that keep to these rules, and one draw needn't show every extreme that they name: `prefix_of`: among the 32 requests of one blk index b, at most 2 name the same holder group.
All inputs are finite; a program needn't handle non-finite values. No bound on the sum of `suffix_len` on one device may be relied on, other than what follows from the above.
Results may differ from a plain program's by a relative error of at most 0.01.
Values may be sent and summed in bfloat16 or wider, within the bound.
No kernel may reach another device: no remote copies, remote signals or barrier semaphores. Data moves between devices by JAX's collectives and lax.ppermute only.
A program may use at most 64 MiB of HBM per device.

v0:
```python
import functools
import math

import jax
import jax.numpy as jnp
from jax import lax
from jax.experimental import pallas as pl
from jax.experimental.pallas import tpu as pltpu
from jax.sharding import Mesh, PartitionSpec as P

QK_DIM = 192
SCALE = QK_DIM**-0.5
LOG2E = math.log2(math.e)
BF = jnp.bfloat16
F32 = jnp.float32
AXES = ("xh", "z", "c", "y", "xl")
NZ, NY = 8, 4
HEADS, LATENT, ROPE = 64, 512, 64
WIDE = 128
COLS = LATENT // WIDE
LAT_ROWS = COLS * HEADS
Q_ROWS = LAT_ROWS + HEADS // 2
PAIR_ROWS = 2 * LAT_ROWS + 16
OUT_ROWS = LAT_ROWS + 16
NT = (((1,), (1,)), ((), ()))

SMEM = pl.BlockSpec(memory_space=pltpu.SMEM)
VMEM = pl.BlockSpec(memory_space=pltpu.VMEM)

T_ROUTE, T_BACK, T_PICK = 0, 8, 16


def call(kernel, outs, ints, arrays, flops=0, bytes_accessed=0, exps=0):
    single = not isinstance(outs, (list, tuple))
    specs = jax.tree.map(lambda _: VMEM, outs)
    return pl.pallas_call(
        kernel,
        out_shape=outs,
        in_specs=[SMEM] * len(ints) + [VMEM] * len(arrays),
        out_specs=VMEM if single else specs,
        compiler_params=pltpu.CompilerParams(vmem_limit_bytes=48 * 1024 * 1024),
        cost_estimate=pl.CostEstimate(
            flops=flops, bytes_accessed=bytes_accessed, transcendentals=exps
        ),
    )(*ints, *arrays)


def shaped(*shape, dtype=BF):
    return jax.ShapeDtypeStruct(shape, dtype)


def along(x, axis, distance):
    n = lax.axis_size(axis)
    return lax.ppermute(x, axis, [(i, (i + distance) % n) for i in range(n)])


def across(x, flip_xh, flip_xl):
    pairs = [
        (2 * i + j, 2 * (i ^ flip_xh) + (j ^ flip_xl)) for i in range(2) for j in range(2)
    ]
    return lax.ppermute(x, ("xh", "xl"), pairs)


def ranks(dest):
    ids = jnp.arange(dest.shape[0], dtype=jnp.int32)
    before = (ids[None, :] < ids[:, None]) & (dest[None, :] == dest[:, None])
    return jnp.sum(before.astype(jnp.int32), axis=1)


def table(dest, xh, z, c):
    ids = jnp.arange(dest.shape[0], dtype=jnp.int32)
    eight = jnp.arange(8, dtype=jnp.int32)
    cr, xr, slot = eight // 4, (eight // 2) % 2, eight % 2
    rank = ranks(dest)
    holders = ((xh ^ xr) * NZ + z) * 2 + (c ^ cr)
    in_ring = (ids // (2 * NZ) == xh) & (ids % 2 == c)
    match = (dest[None, :] == holders[:, None]) & (rank[None, :] == slot[:, None]) & in_ring[None, :]
    route = jnp.sum(jnp.where(match, (ids[None, :] // 2) % NZ + 1, 0), axis=1) - 1
    roots = (xh * NZ + eight) * 2 + c
    root = roots[:, None] == ids[None, :]
    h = jnp.sum(jnp.where(root, dest[None], 0), axis=1)
    r = jnp.sum(jnp.where(root, rank[None], 0), axis=1)
    place = ((h % 2) ^ c) * 4 + ((h // (2 * NZ)) ^ xh) * 2 + r
    back = jnp.where((h // 2) % NZ == z, place, -1)
    mine = eight == z
    pick = jnp.stack([jnp.sum(jnp.where(mine, (h // 2) % NZ, 0)), jnp.sum(jnp.where(mine, r, 0))])
    return jnp.concatenate([route, back, pick]).astype(jnp.int32)


def route_kernel(first, t, heard, keep, send):
    for slot in range(8):
        out = (keep if slot < 4 else send).at[slot % 4]
        source = t[T_ROUTE + slot]

        @pl.when(source >= 0)
        def _():
            out[...] = heard[source, first : first + Q_ROWS]

        @pl.when(source < 0)
        def _():
            out[...] = jnp.zeros(out.shape, BF)


def merge_c_kernel(keep, got, near, far):
    for r in range(2):
        near[r] = keep[r] + got[r]
        far[r] = keep[2 + r] + got[2 + r]


def merge_x_kernel(near, from_xl, from_xh, from_both, out):
    for r in range(2):
        out[r] = near[r] + from_xh[r]
        out[2 + r] = from_xl[r] + from_both[r]


def queries_of(units):
    lat, rot = [], []
    lanes = lax.broadcasted_iota(jnp.int32, (HEADS // 2, WIDE), 1)
    for u in units:
        lat.append(
            jnp.concatenate([u[HEADS * j : HEADS * (j + 1)] for j in range(COLS)], axis=1)
        )
        pair = u[LAT_ROWS:Q_ROWS]
        zero = jnp.zeros_like(pair)
        rot += [jnp.where(lanes < ROPE, pair, zero), jnp.where(lanes < ROPE, zero, pair)]
    return jnp.concatenate(lat, axis=0), jnp.concatenate(rot, axis=0)


def prefix_kernel(q0, q1, q2, q3, keys, rope, o0, o1, o2, o3, rope2):
    rope2[:ROPE] = rope[...]
    rope2[ROPE:] = rope[...]
    for q, o in ((q0, o0), (q1, o1), (q2, o2), (q3, o3)):
        lat, rot = queries_of([q[u] for u in range(4)])
        s = lax.dot_general(lat, keys[...], NT, preferred_element_type=F32)
        s = s + jnp.dot(rot, rope2[...], preferred_element_type=F32)
        top = jnp.max(s, axis=1, keepdims=True)
        w = jnp.exp2((s - top) * (SCALE * LOG2E))
        total = jnp.sum(w, axis=1, keepdims=True)
        out = jnp.dot(w.astype(BF), keys[...], preferred_element_type=F32)
        out = (out / total).astype(BF)
        lse = top * SCALE + jnp.log(total)
        flat = jnp.transpose(jnp.broadcast_to(lse, (4 * HEADS, WIDE)))
        for u in range(4):
            for j in range(COLS):
                at = (u % 2) * LAT_ROWS + j * HEADS
                o[u // 2, at : at + HEADS] = out[
                    u * HEADS : (u + 1) * HEADS, j * WIDE : (j + 1) * WIDE
                ]
        for t in range(2):
            o[t, 2 * LAT_ROWS :] = in_thirds(flat[0:1, t * WIDE : (t + 1) * WIDE])


def in_thirds(row):
    high = row.astype(BF).astype(F32)
    mid = (row - high).astype(BF).astype(F32)
    low = row - high - mid
    place = lax.broadcasted_iota(jnp.int32, (16, WIDE), 0)
    block = jnp.where(place == 0, high, jnp.where(place == 1, mid, jnp.where(place == 2, low, 0.0)))
    return block.astype(BF)


def from_thirds(block):
    block = block.astype(F32)
    return block[0:1] + block[1:2] + block[2:3]


def down(row):
    return jnp.transpose(jnp.broadcast_to(row, (WIDE, WIDE)))


def merge_parts(parts, out):
    lses = [from_thirds(p[2 * LAT_ROWS :]) for p in parts]
    top = functools.reduce(jnp.maximum, lses)
    shares = [jnp.exp(x - top) for x in lses]
    total = functools.reduce(jnp.add, shares)
    weights = [down(x / total) for x in shares]
    for r in range(2):
        ws = [w[r * HEADS : (r + 1) * HEADS] for w in weights]
        for j in range(COLS):
            at = r * LAT_ROWS + j * HEADS
            mixed = [w * p[at : at + HEADS].astype(F32) for w, p in zip(ws, parts)]
            out[at : at + HEADS] = functools.reduce(jnp.add, mixed).astype(BF)
    out[2 * LAT_ROWS :] = in_thirds(top + jnp.log(total))


def merge_y_kernel(p0, p1, p2, p3, near, far):
    for t, out in ((0, near), (1, far)):
        merge_parts([p.at[t] for p in (p0, p1, p2, p3)], out)


def merge_xl_kernel(near, from_xl, from_xh, from_both, out):
    merge_parts([near, from_xl], out.at[0])
    merge_parts([from_xh, from_both], out.at[1])


def back_kernel(t, own, got, out):
    for d in range(NZ):
        place = t[T_BACK + d]
        for k in range(8):

            @pl.when(place == k)
            def _():
                pair = (got if k // 4 else own).at[(k // 2) % 2]
                at = (k % 2) * LAT_ROWS
                out[d, :LAT_ROWS] = pair[at : at + LAT_ROWS]
                out[d, LAT_ROWS:] = pair[2 * LAT_ROWS :]

        @pl.when(place < 0)
        def _():
            out[d] = jnp.zeros((OUT_ROWS, WIDE), BF)


def suffix_kernel(length, units, keys, rope, out, out_lse, rope2):
    rope2[:ROPE] = rope[...]
    rope2[ROPE:] = rope[...]
    lat, rot = queries_of([units[0], units[1]])
    s = lax.dot_general(lat, keys[...], NT, preferred_element_type=F32)
    s = (s + jnp.dot(rot, rope2[...], preferred_element_type=F32)) * SCALE
    position = lax.broadcasted_iota(jnp.int32, s.shape, 1)
    step = lax.broadcasted_iota(jnp.int32, s.shape, 0) // HEADS
    s = jnp.where(position < length[0] + step + 1, s, -1e30)
    top = jnp.max(s, axis=1, keepdims=True)
    w = jnp.exp(s - top)
    total = jnp.sum(w, axis=1, keepdims=True)
    out[...] = jnp.dot(w.astype(BF), keys[...], preferred_element_type=F32) / total
    out_lse[...] = jnp.broadcast_to(top + jnp.log(total), out_lse.shape)


def final_kernel(step, t, units, suffix, suffix_lse, out):
    held = units.at[t[T_PICK] if units.shape[0] > 1 else 0]
    lses = down(from_thirds(held[LAT_ROWS:]))
    pre = jnp.where(t[T_PICK + 1] == 1, lses[HEADS:], lses[:HEADS])
    rows = slice(step * HEADS, (step + 1) * HEADS)
    suf = suffix_lse[rows]
    top = jnp.maximum(pre, suf)
    w_pre, w_suf = jnp.exp(pre - top), jnp.exp(suf - top)
    total = w_pre + w_suf
    for j in range(COLS):
        got = held[j * HEADS : (j + 1) * HEADS].astype(F32)
        cols = slice(j * WIDE, (j + 1) * WIDE)
        out[:, cols] = ((w_pre * got + w_suf * suffix[rows, cols]) / total).astype(BF)


def body(
    q_latent, q_rope, prefix_latent, prefix_rope, suffix_latent, suffix_rope, prefix_of, suffix_len
):
    steps = q_latent.shape[1]
    xh, z, c = (lax.axis_index(a) for a in ("xh", "z", "c"))
    lat = q_latent[0].reshape(steps, HEADS, COLS, WIDE).transpose(0, 2, 1, 3)
    rot = q_rope[0].reshape(steps, 2, HEADS // 2, ROPE).transpose(0, 2, 1, 3)
    units = jnp.concatenate(
        [lat.reshape(steps, LAT_ROWS, WIDE), rot.reshape(steps, HEADS // 2, WIDE)], axis=1
    )
    t = table(prefix_of[0, :, 0], xh, z, c)
    keys, rope = prefix_latent[0], prefix_rope[0]
    positions = keys.shape[0]

    rows = steps * HEADS
    suffix, suffix_lse = pl.pallas_call(
        suffix_kernel,
        out_shape=[shaped(rows, LATENT, dtype=F32), shaped(rows, WIDE, dtype=F32)],
        in_specs=[SMEM, VMEM, VMEM, VMEM],
        out_specs=[VMEM, VMEM],
        scratch_shapes=[pltpu.VMEM((2 * ROPE, positions), BF)],
        compiler_params=pltpu.CompilerParams(vmem_limit_bytes=48 * 1024 * 1024),
        cost_estimate=pl.CostEstimate(
            flops=2 * rows * 2048 * 1152, bytes_accessed=3 << 20, transcendentals=rows * 2048
        ),
    )(suffix_len, units, suffix_latent[0], suffix_rope[0])

    heard_all = lax.all_gather(units.reshape(steps * Q_ROWS, WIDE), "z")
    ahead = jnp.broadcast_to(units[0][None], (NZ, Q_ROWS, WIDE))
    heard_first = lax.all_to_all(ahead, "z", 0, 0, tiled=True)

    def chunk(step):
        heard, first = (heard_first, 0) if step == 0 else (heard_all, step * Q_ROWS)
        quad = shaped(4, Q_ROWS, WIDE)
        pair_q = shaped(2, Q_ROWS, WIDE)
        keep, send = call(
            functools.partial(route_kernel, first), [quad, quad], [t], [heard], bytes_accessed=1 << 20
        )
        got = along(send, "c", 1)
        near, far = call(merge_c_kernel, [pair_q, pair_q], [], [keep, got], bytes_accessed=1 << 20)
        mine = call(
            merge_x_kernel,
            quad,
            [],
            [near, across(near, 0, 1), across(far, 1, 0), across(far, 1, 1)],
            bytes_accessed=1 << 20,
        )
        asked = [mine] + [along(mine, "y", d) for d in range(1, NY)]
        pairs = shaped(2, PAIR_ROWS, WIDE)
        parts = pl.pallas_call(
            prefix_kernel,
            out_shape=[pairs] * NY,
            in_specs=[VMEM] * (NY + 2),
            out_specs=[VMEM] * NY,
            scratch_shapes=[pltpu.VMEM((2 * ROPE, positions), BF)],
            compiler_params=pltpu.CompilerParams(vmem_limit_bytes=48 * 1024 * 1024),
            cost_estimate=pl.CostEstimate(
                flops=2 * 1024 * 2048 * 1152, bytes_accessed=6 << 20, transcendentals=1024 * 2048
            ),
        )(*asked, keys, rope)
        back = [parts[0]] + [along(parts[d], "y", -d) for d in range(1, NY)]
        pair = shaped(PAIR_ROWS, WIDE)
        p_near, p_far = call(merge_y_kernel, [pair, pair], [], back, bytes_accessed=1 << 20)
        both = call(
            merge_xl_kernel,
            pairs,
            [],
            [p_near, across(p_far, 0, 1), across(p_near, 1, 0), across(p_far, 1, 1)],
            bytes_accessed=1 << 20,
        )
        out = call(
            back_kernel,
            shaped(NZ, OUT_ROWS, WIDE),
            [t],
            [both, along(both, "c", 1)],
            bytes_accessed=1 << 20,
        )
        if step == 0:
            arrived = lax.psum_scatter(out, "z", scatter_dimension=0, tiled=True)
        else:
            arrived = lax.all_to_all(out, "z", 0, 0, tiled=True)
        return call(
            functools.partial(final_kernel, step),
            shaped(HEADS, LATENT),
            [t],
            [arrived, suffix, suffix_lse],
            bytes_accessed=1 << 20,
        )

    return jnp.stack([chunk(step) for step in range(steps)])[None]


def solution(mesh):
    fine = Mesh(mesh.devices.reshape(2, NZ, 2, NY, 2), AXES)
    grp, blk = ("xh", "z", "c"), ("y", "xl")
    in_specs = (
        P(AXES, None, None, None),
        P(AXES, None, None),
        P(grp, blk, None),
        P(grp, None, blk),
        P(AXES, None, None),
        P(AXES, None, None),
        P(blk, None, None),
        P(AXES),
    )
    return jax.shard_map(
        body, mesh=fine, in_specs=in_specs, out_specs=P(AXES, None, None, None), check_vma=False
    )
```

profile of v0, /device:TPU:8, one launch (start us, length us, event | category | flops | bytes accessed | tf_op | source)
XLA Modules:
  0.0 204.5 jit_solution(1107557419384662644)
XLA Ops:
  6.5 0.8 reshape_squeeze.7
  7.5 0.9 reshape_squeeze.6
  9.2 0.9 broadcast_in_dim.47
  10.1 8.6 %all-to-all-start = ((bf16[8,288,128]{2,1,0:T(8,128)(2,1)}), bf16[8,288,128]{2,1,0:T(8,128)(2,1)S(1)}, u32[]{:S(2)}, u32[]{:S(2)}) async-start(bf16[8,288,128]{2,1,0:T(8,128)(2,1)} %broadcast_in_dim.47), calls=%async_computation | async-start | bytes 1179648 | tf_op jit(solution)/shard_map/all_to_all | solution.py:273
  20.5 1.3 pad_add_fusion.t
  21.8 20.1 %all-to-all-done.heard = bf16[8,288,128]{2,1,0:T(8,128)(2,1)S(1)} async-done(((bf16[8,288,128]{2,1,0:T(8,128)(2,1)}), bf16[8,288,128]{2,1,0:T(8,128)(2,1)S(1)}, u32[]{:S(2)}, u32[]{:S(2)}) %all-to-all-start) | async-done | bytes 589856 | tf_op jit(solution)/shard_map/all_to_all | solution.py:273
  42.8 1.6 collective-permute-done.got
  44.4 1.6 collective-permute-start.1
  46.0 2.1 %collective-permute-start.3 = (bf16[2,288,128]{2,1,0:T(8,128)(2,1)S(1)}, bf16[2,288,128]{2,1,0:T(8,128)(2,1)S(1)}, u32[]{:S(2)}, u32[]{:S(2)}) collective-permute-start(bf16[2,288,128]{2,1,0:T(8,128)(2,1)S(1)} %get-tuple-element.30), channel_id=1, source_target_pairs={{0,129},{1,128},{128,1},{129,0},{2,131},{3,130},{130,3},{131,2},{4... | collective-permute-start | bytes 442376 | tf_op jit(solution)/shard_map/ppermute | solution.py:61
  48.8 1.7 collective-permute-done.1.from_xl
  50.5 5.5 %collective-permute-done.3.from_both = bf16[2,288,128]{2,1,0:T(8,128)(2,1)S(1)} collective-permute-done((bf16[2,288,128]{2,1,0:T(8,128)(2,1)S(1)}, bf16[2,288,128]{2,1,0:T(8,128)(2,1)S(1)}, u32[]{:S(2)}, u32[]{:S(2)}) %collective-permute-start.3) | collective-permute-done | bytes 147488 | tf_op jit(solution)/shard_map/ppermute | solution.py:61
  56.5 2.7 %collective-permute-start.5 = (bf16[4,288,128]{2,1,0:T(8,128)(2,1)S(1)}, bf16[4,288,128]{2,1,0:T(8,128)(2,1)S(1)}, u32[]{:S(2)}, u32[]{:S(2)}) collective-permute-start(bf16[4,288,128]{2,1,0:T(8,128)(2,1)S(1)} %shard_map.84.q0), channel_id=1, source_target_pairs={{0,4},{2,6},{4,0},{6,2},{1,5},{3,7},{5,1},{7,3},{8,12},{10,14},{12... | collective-permute-start | bytes 884744 | tf_op jit(solution)/shard_map/ppermute | solution.py:54
  59.2 1.9 collective-permute-start.4
  61.2 1.3 copy-done.2
  63.2 1.8 collective-permute-done.6.q3
  65.0 6.6 %collective-permute-done.5.q2 = bf16[4,288,128]{2,1,0:T(8,128)(2,1)S(1)} collective-permute-done((bf16[4,288,128]{2,1,0:T(8,128)(2,1)S(1)}, bf16[4,288,128]{2,1,0:T(8,128)(2,1)S(1)}, u32[]{:S(2)}, u32[]{:S(2)}) %collective-permute-start.5) | collective-permute-done | bytes 294944 | tf_op jit(solution)/shard_map/ppermute | solution.py:54
  71.6 0.9 collective-permute-done.4.q1
  72.5 0.9 copy-done.6
  73.4 7.6 %shard_map.85 = (bf16[2,528,128]{2,1,0:T(8,128)(2,1)S(1)}, bf16[2,528,128]{2,1,0:T(8,128)(2,1)S(1)}, bf16[2,528,128]{2,1,0:T(8,128)(2,1)S(1)}, bf16[2,528,128]{2,1,0:T(8,128)(2,1)S(1)}) custom-call(bf16[4,288,128]{2,1,0:T(8,128)(2,1)S(1)} %shard_map.84.q0, bf16[4,288,128]{2,1,0:T(8,128)(2,1)} %collective-permute-done.4.q1, ...), custom_call_target="tpu_custom_call" | custom-call | flops 4831838208 | bytes 6291456 | tf_op jit(solution)/shard_map/pallas_call | solution.py:293
  81.0 3.2 %collective-permute-start.7 = (bf16[2,528,128]{2,1,0:T(8,128)(2,1)S(1)}, bf16[2,528,128]{2,1,0:T(8,128)(2,1)S(1)}, u32[]{:S(2)}, u32[]{:S(2)}) collective-permute-start(bf16[2,528,128]{2,1,0:T(8,128)(2,1)S(1)} %get-tuple-element.32), channel_id=1, source_target_pairs={{0,6},{2,0},{4,2},{6,4},{1,7},{3,1},{5,3},{7,5},{8,14},{10,8},{12,... | collective-permute-start | bytes 811016 | tf_op jit(solution)/shard_map/ppermute | solution.py:54
  84.4 2.0 collective-permute-start.17
  86.4 2.0 %collective-permute-start.16 = (bf16[2,288,128]{2,1,0:T(8,128)(2,1)S(1)}, bf16[2,288,128]{2,1,0:T(8,128)(2,1)S(1)}, u32[]{:S(2)}, u32[]{:S(2)}) collective-permute-start(bf16[2,288,128]{2,1,0:T(8,128)(2,1)S(1)} %get-tuple-element.42), channel_id=1, source_target_pairs={{0,128},{1,129},{128,0},{129,1},{2,130},{3,131},{130,2},{131,3},{4... | collective-permute-start | bytes 442376 | tf_op jit(solution)/shard_map/ppermute | solution.py:61
  88.5 2.6 %collective-permute-done.15.from_xl = bf16[2,288,128]{2,1,0:T(8,128)(2,1)S(1)} collective-permute-done((bf16[2,288,128]{2,1,0:T(8,128)(2,1)S(1)}, bf16[2,288,128]{2,1,0:T(8,128)(2,1)S(1)}, u32[]{:S(2)}, u32[]{:S(2)}) %collective-permute-start.15) | collective-permute-done | bytes 147488 | tf_op jit(solution)/shard_map/ppermute | solution.py:61
  91.1 1.5 collective-permute-done.17.from_both
  92.6 1.8 collective-permute-done.16.from_xh
  94.9 2.3 %collective-permute-start.18 = (bf16[4,288,128]{2,1,0:T(8,128)(2,1)S(1)}, bf16[4,288,128]{2,1,0:T(8,128)(2,1)S(1)}, u32[]{:S(2)}, u32[]{:S(2)}) collective-permute-start(bf16[4,288,128]{2,1,0:T(8,128)(2,1)S(1)} %shard_map.93.q0), channel_id=1, source_target_pairs={{0,2},{2,4},{4,6},{6,0},{1,3},{3,5},{5,7},{7,1},{8,10},{10,12},{12... | collective-permute-start | bytes 884744 | tf_op jit(solution)/shard_map/ppermute | solution.py:54
  97.3 3.5 %collective-permute-start.8 = (bf16[2,528,128]{2,1,0:T(8,128)(2,1)S(1)}, bf16[2,528,128]{2,1,0:T(8,128)(2,1)S(1)}, u32[]{:S(2)}, u32[]{:S(2)}) collective-permute-start(bf16[2,528,128]{2,1,0:T(8,128)(2,1)S(1)} %get-tuple-element.33), channel_id=1, source_target_pairs={{0,4},{2,6},{4,0},{6,2},{1,5},{3,7},{5,1},{7,3},{8,12},{10,14},{12... | collective-permute-start | bytes 811016 | tf_op jit(solution)/shard_map/ppermute | solution.py:54
  100.7 12.1 %collective-permute-done.8.p2 = bf16[2,528,128]{2,1,0:T(8,128)(2,1)S(1)} collective-permute-done((bf16[2,528,128]{2,1,0:T(8,128)(2,1)S(1)}, bf16[2,528,128]{2,1,0:T(8,128)(2,1)S(1)}, u32[]{:S(2)}, u32[]{:S(2)}) %collective-permute-start.8) | collective-permute-done | bytes 270368 | tf_op jit(solution)/shard_map/ppermute | solution.py:54
  112.9 9.3 %collective-permute-done.9.p3 = bf16[2,528,128]{2,1,0:T(8,128)(2,1)S(1)} collective-permute-done((bf16[2,528,128]{2,1,0:T(8,128)(2,1)S(1)}, bf16[2,528,128]{2,1,0:T(8,128)(2,1)S(1)}, u32[]{:S(2)}, u32[]{:S(2)}) %collective-permute-start.9) | collective-permute-done | bytes 270368 | tf_op jit(solution)/shard_map/ppermute | solution.py:54
  122.6 6.6 %shard_map.94 = (bf16[2,528,128]{2,1,0:T(8,128)(2,1)S(1)}, bf16[2,528,128]{2,1,0:T(8,128)(2,1)S(1)}, bf16[2,528,128]{2,1,0:T(8,128)(2,1)S(1)}, bf16[2,528,128]{2,1,0:T(8,128)(2,1)S(1)}) custom-call(bf16[4,288,128]{2,1,0:T(8,128)(2,1)S(1)} %shard_map.93.q0, bf16[4,288,128]{2,1,0:T(8,128)(2,1)S(1)} %collective-permute-done.18.q1, ...), custom_call_target="tpu_custom_call" | custom-call | flops 4831838208 | bytes 6291456 | tf_op jit(solution)/shard_map/pallas_call | solution.py:293
  129.9 1.1 collective-permute-start.22
  131.1 0.9 collective-permute-start.23
  132.0 2.0 collective-permute-start.12
  134.0 1.4 collective-permute-start.10
  135.4 2.8 %collective-permute-done.12.from_both = bf16[528,128]{1,0:T(8,128)(2,1)S(1)} collective-permute-done((bf16[528,128]{1,0:T(8,128)(2,1)S(1)}, bf16[528,128]{1,0:T(8,128)(2,1)S(1)}, u32[]{:S(2)}, u32[]{:S(2)}) %collective-permute-start.12) | collective-permute-done | bytes 135200 | tf_op jit(solution)/shard_map/ppermute | solution.py:61
  138.2 0.8 collective-permute-done.10.from_xl
  139.3 2.6 %collective-permute-done.22.p2 = bf16[2,528,128]{2,1,0:T(8,128)(2,1)S(1)} collective-permute-done((bf16[2,528,128]{2,1,0:T(8,128)(2,1)S(1)}, bf16[2,528,128]{2,1,0:T(8,128)(2,1)S(1)}, u32[]{:S(2)}, u32[]{:S(2)}) %collective-permute-start.22) | collective-permute-done | bytes 270368 | tf_op jit(solution)/shard_map/ppermute | solution.py:54
  142.0 1.1 collective-permute-done.23.p3
  143.3 3.3 %collective-permute-start.25 = (bf16[528,128]{1,0:T(8,128)(2,1)S(1)}, bf16[528,128]{1,0:T(8,128)(2,1)S(1)}, u32[]{:S(2)}, u32[]{:S(2)}) collective-permute-start(bf16[528,128]{1,0:T(8,128)(2,1)S(1)} %get-tuple-element.47.near), channel_id=1, source_target_pairs={{0,128},{1,129},{128,0},{129,1},{2,130},{3,131},{130,2},{131,3},{4... | collective-permute-start | bytes 405512 | tf_op jit(solution)/shard_map/ppermute | solution.py:61
  146.6 1.0 collective-permute-start.26
  147.7 2.4 %collective-permute-done.25.from_xh = bf16[528,128]{1,0:T(8,128)(2,1)S(1)} collective-permute-done((bf16[528,128]{1,0:T(8,128)(2,1)S(1)}, bf16[528,128]{1,0:T(8,128)(2,1)S(1)}, u32[]{:S(2)}, u32[]{:S(2)}) %collective-permute-start.25) | collective-permute-done | bytes 135200 | tf_op jit(solution)/shard_map/ppermute | solution.py:61
  150.1 2.8 %collective-permute-done.26.from_both = bf16[528,128]{1,0:T(8,128)(2,1)S(1)} collective-permute-done((bf16[528,128]{1,0:T(8,128)(2,1)S(1)}, bf16[528,128]{1,0:T(8,128)(2,1)S(1)}, u32[]{:S(2)}, u32[]{:S(2)}) %collective-permute-start.26) | collective-permute-done | bytes 135200 | tf_op jit(solution)/shard_map/ppermute | solution.py:61
  153.2 1.8 shard_map.88
  155.0 1.8 shard_map.97
  156.8 3.5 %all-to-all-start.1 = ((bf16[8,272,128]{2,1,0:T(8,128)(2,1)}), bf16[8,272,128]{2,1,0:T(8,128)(2,1)S(1)}, u32[]{:S(2)}, u32[]{:S(2)}) async-start(bf16[8,272,128]{2,1,0:T(8,128)(2,1)} %shard_map.97), calls=%async_computation.2 | async-start | bytes 1114112 | tf_op jit(solution)/shard_map/all_to_all | solution.py:324
  161.0 1.6 shard_map.89
  162.6 32.2 %reduce-scatter.2.cloned.1.call-done.units = bf16[1,272,128]{2,1,0:T(8,128)(2,1)} async-done(((bf16[8,272,128]{2,1,0:T(8,128)(2,1)}), bf16[1,272,128]{2,1,0:T(8,128)(2,1)}) %reduce-scatter.2.cloned.1.call-update) | async-done | bytes 69648 | tf_op jit(solution)/shard_map/reduce_scatter | solution.py:322
  194.8 0.9 copy-done.4
  (72 shorter events, 10.1 us)
Async XLA Ops:
  6.5 12.3 %copy-start.8 = (s32[1,32,1]{1,2,0:T(1,128)S(1)}, s32[1,32,1]{1,2,0:T(1,128)}, u32[]{:S(2)}) copy-start(s32[1,32,1]{1,2,0:T(1,128)} %param.14) | copy-start | bytes 388
  6.5 54.6 %all-gather.2.cloned.1.call-start = ((), (), s32[]{:S(2)}) async-start(), calls=%async_computation.4 | async-start | bytes 1327104 | tf_op jit(solution)/shard_map/all_gather | solution.py:271
  10.1 62.4 %copy-start.5 = (bf16[1,2048,512]{2,1,0:T(8,128)(2,1)S(1)}, bf16[1,2048,512]{2,1,0:T(8,128)(2,1)}, u32[]{:S(2)}) copy-start(bf16[1,2048,512]{2,1,0:T(8,128)(2,1)} %param.10) | copy-start | bytes 6291460
  10.1 31.9 %all-to-all-start = ((bf16[8,288,128]{2,1,0:T(8,128)(2,1)}), bf16[8,288,128]{2,1,0:T(8,128)(2,1)S(1)}, u32[]{:S(2)}, u32[]{:S(2)}) async-start(bf16[8,288,128]{2,1,0:T(8,128)(2,1)} %broadcast_in_dim.47), calls=%async_computation | async-start | bytes 1179648 | tf_op jit(solution)/shard_map/all_to_all | solution.py:273
  18.7 176.1 %reduce-scatter.2.cloned.1.call-start = ((), (), s32[]{:S(2)}) async-start(), calls=%async_computation.3 | async-start | bytes 626688 | tf_op jit(solution)/shard_map/reduce_scatter | solution.py:322
  42.7 1.7 collective-permute-start
  44.4 6.1 %collective-permute-start.1 = (bf16[2,288,128]{2,1,0:T(8,128)(2,1)S(1)}, bf16[2,288,128]{2,1,0:T(8,128)(2,1)S(1)}, u32[]{:S(2)}, u32[]{:S(2)}) collective-permute-start(bf16[2,288,128]{2,1,0:T(8,128)(2,1)S(1)} %get-tuple-element.29.near), channel_id=1, source_target_pairs={{0,1},{1,0},{128,129},{129,128},{2,3},{3,2},{130,131},{131,130},{4... | collective-permute-start | bytes 442376 | tf_op jit(solution)/shard_map/ppermute | solution.py:61
  46.0 10.0 %collective-permute-start.3 = (bf16[2,288,128]{2,1,0:T(8,128)(2,1)S(1)}, bf16[2,288,128]{2,1,0:T(8,128)(2,1)S(1)}, u32[]{:S(2)}, u32[]{:S(2)}) collective-permute-start(bf16[2,288,128]{2,1,0:T(8,128)(2,1)S(1)} %get-tuple-element.30), channel_id=1, source_target_pairs={{0,129},{1,128},{128,1},{129,0},{2,131},{3,130},{130,3},{131,2},{4... | collective-permute-start | bytes 442376 | tf_op jit(solution)/shard_map/ppermute | solution.py:61
  48.1 7.9 %collective-permute-start.2 = (bf16[2,288,128]{2,1,0:T(8,128)(2,1)S(1)}, bf16[2,288,128]{2,1,0:T(8,128)(2,1)S(1)}, u32[]{:S(2)}, u32[]{:S(2)}) collective-permute-start(bf16[2,288,128]{2,1,0:T(8,128)(2,1)S(1)} %get-tuple-element.30), channel_id=1, source_target_pairs={{0,128},{1,129},{128,0},{129,1},{2,130},{3,131},{130,2},{131,3},{4... | collective-permute-start | bytes 442376 | tf_op jit(solution)/shard_map/ppermute | solution.py:61
  56.1 8.9 %collective-permute-start.6 = (bf16[4,288,128]{2,1,0:T(8,128)(2,1)S(1)}, bf16[4,288,128]{2,1,0:T(8,128)(2,1)S(1)}, u32[]{:S(2)}, u32[]{:S(2)}) collective-permute-start(bf16[4,288,128]{2,1,0:T(8,128)(2,1)S(1)} %shard_map.84.q0), channel_id=1, source_target_pairs={{0,6},{2,0},{4,2},{6,4},{1,7},{3,1},{5,3},{7,5},{8,14},{10,8},{12,... | collective-permute-start | bytes 884744 | tf_op jit(solution)/shard_map/ppermute | solution.py:54
  56.5 15.1 %collective-permute-start.5 = (bf16[4,288,128]{2,1,0:T(8,128)(2,1)S(1)}, bf16[4,288,128]{2,1,0:T(8,128)(2,1)S(1)}, u32[]{:S(2)}, u32[]{:S(2)}) collective-permute-start(bf16[4,288,128]{2,1,0:T(8,128)(2,1)S(1)} %shard_map.84.q0), channel_id=1, source_target_pairs={{0,4},{2,6},{4,0},{6,2},{1,5},{3,7},{5,1},{7,3},{8,12},{10,14},{12... | collective-permute-start | bytes 884744 | tf_op jit(solution)/shard_map/ppermute | solution.py:54
  59.2 13.2 %collective-permute-start.4 = (bf16[4,288,128]{2,1,0:T(8,128)(2,1)S(1)}, bf16[4,288,128]{2,1,0:T(8,128)(2,1)}, u32[]{:S(2)}, u32[]{:S(2)}) collective-permute-start(bf16[4,288,128]{2,1,0:T(8,128)(2,1)S(1)} %shard_map.84.q0), channel_id=1, source_target_pairs={{0,2},{2,4},{4,6},{6,0},{1,3},{3,5},{5,7},{7,1},{8,10},{10,12},{12... | collective-permute-start | bytes 884744 | tf_op jit(solution)/shard_map/ppermute | solution.py:54
  61.2 1.3 copy-start.2
  63.1 21.1 %collective-permute-start.14 = (bf16[4,288,128]{2,1,0:T(8,128)(2,1)S(1)}, bf16[4,288,128]{2,1,0:T(8,128)(2,1)S(1)}, u32[]{:S(2)}, u32[]{:S(2)}) collective-permute-start(bf16[4,288,128]{2,1,0:T(8,128)(2,1)S(1)} %get-tuple-element.40), channel_id=1, source_target_pairs={{0,8},{8,0},{1,9},{9,1},{2,10},{10,2},{3,11},{11,3},{4,12},{12,4},... | collective-permute-start | bytes 884744 | tf_op jit(solution)/shard_map/ppermute | solution.py:54
  72.5 1.0 copy-start.6
  81.0 41.6 %copy-start.7 = (bf16[1,64,2048]{2,1,0:T(8,128)(2,1)S(1)}, bf16[1,64,2048]{2,1,0:T(8,128)(2,1)}, u32[]{:S(2)}) copy-start(bf16[1,64,2048]{2,1,0:T(8,128)(2,1)} %param.11) | copy-start | bytes 786436
  81.0 19.7 %collective-permute-start.7 = (bf16[2,528,128]{2,1,0:T(8,128)(2,1)S(1)}, bf16[2,528,128]{2,1,0:T(8,128)(2,1)S(1)}, u32[]{:S(2)}, u32[]{:S(2)}) collective-permute-start(bf16[2,528,128]{2,1,0:T(8,128)(2,1)S(1)} %get-tuple-element.32), channel_id=1, source_target_pairs={{0,6},{2,0},{4,2},{6,4},{1,7},{3,1},{5,3},{7,5},{8,14},{10,8},{12,... | collective-permute-start | bytes 811016 | tf_op jit(solution)/shard_map/ppermute | solution.py:54
  84.3 6.8 %collective-permute-start.15 = (bf16[2,288,128]{2,1,0:T(8,128)(2,1)S(1)}, bf16[2,288,128]{2,1,0:T(8,128)(2,1)S(1)}, u32[]{:S(2)}, u32[]{:S(2)}) collective-permute-start(bf16[2,288,128]{2,1,0:T(8,128)(2,1)S(1)} %get-tuple-element.41.near), channel_id=1, source_target_pairs={{0,1},{1,0},{128,129},{129,128},{2,3},{3,2},{130,131},{131,130},{4... | collective-permute-start | bytes 442376 | tf_op jit(solution)/shard_map/ppermute | solution.py:61
  84.4 8.3 %collective-permute-start.17 = (bf16[2,288,128]{2,1,0:T(8,128)(2,1)S(1)}, bf16[2,288,128]{2,1,0:T(8,128)(2,1)S(1)}, u32[]{:S(2)}, u32[]{:S(2)}) collective-permute-start(bf16[2,288,128]{2,1,0:T(8,128)(2,1)S(1)} %get-tuple-element.42), channel_id=1, source_target_pairs={{0,129},{1,128},{128,1},{129,0},{2,131},{3,130},{130,3},{131,2},{4... | collective-permute-start | bytes 442376 | tf_op jit(solution)/shard_map/ppermute | solution.py:61
  86.4 8.0 %collective-permute-start.16 = (bf16[2,288,128]{2,1,0:T(8,128)(2,1)S(1)}, bf16[2,288,128]{2,1,0:T(8,128)(2,1)S(1)}, u32[]{:S(2)}, u32[]{:S(2)}) collective-permute-start(bf16[2,288,128]{2,1,0:T(8,128)(2,1)S(1)} %get-tuple-element.42), channel_id=1, source_target_pairs={{0,128},{1,129},{128,0},{129,1},{2,130},{3,131},{130,2},{131,3},{4... | collective-permute-start | bytes 442376 | tf_op jit(solution)/shard_map/ppermute | solution.py:61
  94.5 28.1 %collective-permute-start.20 = (bf16[4,288,128]{2,1,0:T(8,128)(2,1)S(1)}, bf16[4,288,128]{2,1,0:T(8,128)(2,1)S(1)}, u32[]{:S(2)}, u32[]{:S(2)}) collective-permute-start(bf16[4,288,128]{2,1,0:T(8,128)(2,1)S(1)} %shard_map.93.q0), channel_id=1, source_target_pairs={{0,6},{2,0},{4,2},{6,4},{1,7},{3,1},{5,3},{7,5},{8,14},{10,8},{12,... | collective-permute-start | bytes 884744 | tf_op jit(solution)/shard_map/ppermute | solution.py:54
  94.9 27.7 %collective-permute-start.19 = (bf16[4,288,128]{2,1,0:T(8,128)(2,1)S(1)}, bf16[4,288,128]{2,1,0:T(8,128)(2,1)S(1)}, u32[]{:S(2)}, u32[]{:S(2)}) collective-permute-start(bf16[4,288,128]{2,1,0:T(8,128)(2,1)S(1)} %shard_map.93.q0), channel_id=1, source_target_pairs={{0,4},{2,6},{4,0},{6,2},{1,5},{3,7},{5,1},{7,3},{8,12},{10,14},{12... | collective-permute-start | bytes 884744 | tf_op jit(solution)/shard_map/ppermute | solution.py:54
  94.9 27.6 %collective-permute-start.18 = (bf16[4,288,128]{2,1,0:T(8,128)(2,1)S(1)}, bf16[4,288,128]{2,1,0:T(8,128)(2,1)S(1)}, u32[]{:S(2)}, u32[]{:S(2)}) collective-permute-start(bf16[4,288,128]{2,1,0:T(8,128)(2,1)S(1)} %shard_map.93.q0), channel_id=1, source_target_pairs={{0,2},{2,4},{4,6},{6,0},{1,3},{3,5},{5,7},{7,1},{8,10},{10,12},{12... | collective-permute-start | bytes 884744 | tf_op jit(solution)/shard_map/ppermute | solution.py:54
  97.3 15.6 %collective-permute-start.8 = (bf16[2,528,128]{2,1,0:T(8,128)(2,1)S(1)}, bf16[2,528,128]{2,1,0:T(8,128)(2,1)S(1)}, u32[]{:S(2)}, u32[]{:S(2)}) collective-permute-start(bf16[2,528,128]{2,1,0:T(8,128)(2,1)S(1)} %get-tuple-element.33), channel_id=1, source_target_pairs={{0,4},{2,6},{4,0},{6,2},{1,5},{3,7},{5,1},{7,3},{8,12},{10,14},{12... | collective-permute-start | bytes 811016 | tf_op jit(solution)/shard_map/ppermute | solution.py:54
  100.7 21.4 %collective-permute-start.9 = (bf16[2,528,128]{2,1,0:T(8,128)(2,1)S(1)}, bf16[2,528,128]{2,1,0:T(8,128)(2,1)S(1)}, u32[]{:S(2)}, u32[]{:S(2)}) collective-permute-start(bf16[2,528,128]{2,1,0:T(8,128)(2,1)S(1)} %get-tuple-element.34), channel_id=1, source_target_pairs={{0,2},{2,4},{4,6},{6,0},{1,3},{3,5},{5,7},{7,1},{8,10},{10,12},{12... | collective-permute-start | bytes 811016 | tf_op jit(solution)/shard_map/ppermute | solution.py:54
  122.5 11.6 %collective-permute-start.11 = (bf16[528,128]{1,0:T(8,128)(2,1)S(1)}, bf16[528,128]{1,0:T(8,128)(2,1)S(1)}, u32[]{:S(2)}, u32[]{:S(2)}) collective-permute-start(bf16[528,128]{1,0:T(8,128)(2,1)S(1)} %get-tuple-element.35.near), channel_id=1, source_target_pairs={{0,128},{1,129},{128,0},{129,1},{2,130},{3,131},{130,2},{131,3},{4... | collective-permute-start | bytes 405512 | tf_op jit(solution)/shard_map/ppermute | solution.py:61
  129.2 10.1 %collective-permute-start.21 = (bf16[2,528,128]{2,1,0:T(8,128)(2,1)S(1)}, bf16[2,528,128]{2,1,0:T(8,128)(2,1)S(1)}, u32[]{:S(2)}, u32[]{:S(2)}) collective-permute-start(bf16[2,528,128]{2,1,0:T(8,128)(2,1)S(1)} %get-tuple-element.44), channel_id=1, source_target_pairs={{0,6},{2,0},{4,2},{6,4},{1,7},{3,1},{5,3},{7,5},{8,14},{10,8},{12,... | collective-permute-start | bytes 811016 | tf_op jit(solution)/shard_map/ppermute | solution.py:54
  129.9 12.1 %collective-permute-start.22 = (bf16[2,528,128]{2,1,0:T(8,128)(2,1)S(1)}, bf16[2,528,128]{2,1,0:T(8,128)(2,1)S(1)}, u32[]{:S(2)}, u32[]{:S(2)}) collective-permute-start(bf16[2,528,128]{2,1,0:T(8,128)(2,1)S(1)} %get-tuple-element.45), channel_id=1, source_target_pairs={{0,4},{2,6},{4,0},{6,2},{1,5},{3,7},{5,1},{7,3},{8,12},{10,14},{12... | collective-permute-start | bytes 811016 | tf_op jit(solution)/shard_map/ppermute | solution.py:54
  131.1 12.0 %collective-permute-start.23 = (bf16[2,528,128]{2,1,0:T(8,128)(2,1)S(1)}, bf16[2,528,128]{2,1,0:T(8,128)(2,1)S(1)}, u32[]{:S(2)}, u32[]{:S(2)}) collective-permute-start(bf16[2,528,128]{2,1,0:T(8,128)(2,1)S(1)} %get-tuple-element.46), channel_id=1, source_target_pairs={{0,2},{2,4},{4,6},{6,0},{1,3},{3,5},{5,7},{7,1},{8,10},{10,12},{12... | collective-permute-start | bytes 811016 | tf_op jit(solution)/shard_map/ppermute | solution.py:54
  132.0 6.2 %collective-permute-start.12 = (bf16[528,128]{1,0:T(8,128)(2,1)S(1)}, bf16[528,128]{1,0:T(8,128)(2,1)S(1)}, u32[]{:S(2)}, u32[]{:S(2)}) collective-permute-start(bf16[528,128]{1,0:T(8,128)(2,1)S(1)} %get-tuple-element.36), channel_id=1, source_target_pairs={{0,129},{1,128},{128,1},{129,0},{2,131},{3,130},{130,3},{131,2},{4... | collective-permute-start | bytes 405512 | tf_op jit(solution)/shard_map/ppermute | solution.py:61
  134.0 5.0 %collective-permute-start.10 = (bf16[528,128]{1,0:T(8,128)(2,1)S(1)}, bf16[528,128]{1,0:T(8,128)(2,1)S(1)}, u32[]{:S(2)}, u32[]{:S(2)}) collective-permute-start(bf16[528,128]{1,0:T(8,128)(2,1)S(1)} %get-tuple-element.36), channel_id=1, source_target_pairs={{0,1},{1,0},{128,129},{129,128},{2,3},{3,2},{130,131},{131,130},{4... | collective-permute-start | bytes 405512 | tf_op jit(solution)/shard_map/ppermute | solution.py:61
  139.2 14.0 %collective-permute-start.13 = (bf16[2,528,128]{2,1,0:T(8,128)(2,1)S(1)}, bf16[2,528,128]{2,1,0:T(8,128)(2,1)S(1)}, u32[]{:S(2)}, u32[]{:S(2)}) collective-permute-start(bf16[2,528,128]{2,1,0:T(8,128)(2,1)S(1)} %shard_map.87.own), channel_id=1, source_target_pairs={{0,8},{8,0},{1,9},{9,1},{2,10},{10,2},{3,11},{11,3},{4,12},{12,4},... | collective-permute-start | bytes 811016 | tf_op jit(solution)/shard_map/ppermute | solution.py:54
  143.3 6.7 %collective-permute-start.25 = (bf16[528,128]{1,0:T(8,128)(2,1)S(1)}, bf16[528,128]{1,0:T(8,128)(2,1)S(1)}, u32[]{:S(2)}, u32[]{:S(2)}) collective-permute-start(bf16[528,128]{1,0:T(8,128)(2,1)S(1)} %get-tuple-element.47.near), channel_id=1, source_target_pairs={{0,128},{1,129},{128,0},{129,1},{2,130},{3,131},{130,2},{131,3},{4... | collective-permute-start | bytes 405512 | tf_op jit(solution)/shard_map/ppermute | solution.py:61
  146.6 6.2 %collective-permute-start.26 = (bf16[528,128]{1,0:T(8,128)(2,1)S(1)}, bf16[528,128]{1,0:T(8,128)(2,1)S(1)}, u32[]{:S(2)}, u32[]{:S(2)}) collective-permute-start(bf16[528,128]{1,0:T(8,128)(2,1)S(1)} %get-tuple-element.48), channel_id=1, source_target_pairs={{0,129},{1,128},{128,1},{129,0},{2,131},{3,130},{130,3},{131,2},{4... | collective-permute-start | bytes 405512 | tf_op jit(solution)/shard_map/ppermute | solution.py:61
  147.7 5.2 %collective-permute-start.24 = (bf16[528,128]{1,0:T(8,128)(2,1)S(1)}, bf16[528,128]{1,0:T(8,128)(2,1)S(1)}, u32[]{:S(2)}, u32[]{:S(2)}) collective-permute-start(bf16[528,128]{1,0:T(8,128)(2,1)S(1)} %get-tuple-element.48), channel_id=1, source_target_pairs={{0,1},{1,0},{128,129},{129,128},{2,3},{3,2},{130,131},{131,130},{4... | collective-permute-start | bytes 405512 | tf_op jit(solution)/shard_map/ppermute | solution.py:61
  153.1 7.9 %copy-start = (bf16[1,2048,512]{2,1,0:T(8,128)(2,1)S(1)}, bf16[1,2048,512]{2,1,0:T(8,128)(2,1)}, u32[]{:S(2)}) copy-start(bf16[1,2048,512]{2,1,0:T(8,128)(2,1)} %param.12) | copy-start | bytes 6291460
  153.1 7.9 %copy-start.1 = (bf16[2,288,128]{2,1,0:T(8,128)(2,1)S(1)}, bf16[2,288,128]{2,1,0:T(8,128)(2,1)}, u32[]{:S(2)}) copy-start(bf16[2,288,128]{2,1,0:T(8,128)(2,1)} %pad_maximum_fusion.units) | copy-start | bytes 442372
  153.1 7.9 %copy-start.3 = (bf16[1,64,2048]{2,1,0:T(8,128)(2,1)S(1)}, bf16[1,64,2048]{2,1,0:T(8,128)(2,1)}, u32[]{:S(2)}) copy-start(bf16[1,64,2048]{2,1,0:T(8,128)(2,1)} %param.13) | copy-start | bytes 786436
  153.1 1.9 collective-permute-start.27
  156.8 39.5 %all-to-all-start.1 = ((bf16[8,272,128]{2,1,0:T(8,128)(2,1)}), bf16[8,272,128]{2,1,0:T(8,128)(2,1)S(1)}, u32[]{:S(2)}, u32[]{:S(2)}) async-start(bf16[8,272,128]{2,1,0:T(8,128)(2,1)} %shard_map.97), calls=%async_computation.2 | async-start | bytes 1114112 | tf_op jit(solution)/shard_map/all_to_all | solution.py:324
  194.7 0.9 copy-start.4
Sparse Core Ops, SparseCore 0:
  9.3 45.6 all-gather.1
  155.1 39.5 reduce-scatter.1
where the time goes:
time: 205 us
  waiting for transfers between devices  110 us (54%)
  starting transfers between devices  46.2 us (23%)
  Pallas kernels  23.3 us (11%)
  between operations  14.4 us (7%)
  local copies, waits for them, and re-layouts  5.95 us (3%)
  other arithmetic  4.41 us (2%)
    ppermute x16, waiting for transfers between devices, along(): return lax.ppermute(x, axis, [(i, (i + distance) % n) for i in range(n)])  35.9 us
    reduce_scatter x1, waiting for transfers between devices, chunk(): arrived = lax.psum_scatter(out, 'z', scatter_dimension=0, tiled=True)  32.2 us
    ppermute x12, waiting for transfers between devices, across(): return lax.ppermute(x, ('xh', 'xl'), pairs)  22 us
    all_to_all x1, waiting for transfers between devices, body(): heard_first = lax.all_to_all(ahead, 'z', 0, 0, tiled=True)  20.1 us
    ppermute x16, starting transfers between devices, along(): return lax.ppermute(x, axis, [(i, (i + distance) % n) for i in range(n)])  17.7 us
    ppermute x12, starting transfers between devices, across(): return lax.ppermute(x, ('xh', 'xl'), pairs)  16.3 us
    pallas_call x2, Pallas kernels, chunk(): pl.pallas_call(prefix_kernel, out_shape=[pairs] * NY, in_specs=[VMEM] * (...  14.2 us
    all_to_all x1, starting transfers between devices, body(): heard_first = lax.all_to_all(ahead, 'z', 0, 0, tiled=True)  8.6 us
  transfers between devices with their start and end apart: 32, of which 19 were waited for; matrix products, arithmetic and copies ran while one was open for 2% of the time, Pallas kernels for 11%

commit v1 on v0

v1 whole, which is shorter than its diff:
```python
import functools
import math

import jax
import jax.numpy as jnp
from jax import lax
from jax.experimental import pallas as pl
from jax.experimental.pallas import tpu as pltpu
from jax.sharding import Mesh, PartitionSpec as P

QK_DIM = 192
SCALE = QK_DIM**-0.5
LOG2E = math.log2(math.e)
BF = jnp.bfloat16
F32 = jnp.float32
AXES = ("xh", "z", "c", "y", "xl")
NZ, NY = 8, 4
HEADS, LATENT, ROPE = 64, 512, 64
WIDE = 128
COLS = LATENT // WIDE
ROWS = 2 * HEADS
LAT_ROWS = COLS * ROWS
Q_ROWS = LAT_ROWS + HEADS
HALF = Q_ROWS // 2
OUT_ROWS = LAT_ROWS + 16
NT = (((1,), (1,)), ((), ()))

SMEM = pl.BlockSpec(memory_space=pltpu.SMEM)
VMEM = pl.BlockSpec(memory_space=pltpu.VMEM)

T_ROUTE, T_BACK, T_PICK = 0, 8, 16


def call(kernel, outs, ints, arrays, flops=0, bytes_accessed=0, exps=0):
    single = not isinstance(outs, (list, tuple))
    specs = jax.tree.map(lambda _: VMEM, outs)
    return pl.pallas_call(
        kernel,
        out_shape=outs,
        in_specs=[SMEM] * len(ints) + [VMEM] * len(arrays),
        out_specs=VMEM if single else specs,
        compiler_params=pltpu.CompilerParams(vmem_limit_bytes=48 * 1024 * 1024),
        cost_estimate=pl.CostEstimate(
            flops=flops, bytes_accessed=bytes_accessed, transcendentals=exps
        ),
    )(*ints, *arrays)


def shaped(*shape, dtype=BF):
    return jax.ShapeDtypeStruct(shape, dtype)


def along(x, axis, distance):
    n = lax.axis_size(axis)
    return lax.ppermute(x, axis, [(i, (i + distance) % n) for i in range(n)])


def across(x, flip_xh, flip_xl):
    pairs = [
        (2 * i + j, 2 * (i ^ flip_xh) + (j ^ flip_xl)) for i in range(2) for j in range(2)
    ]
    return lax.ppermute(x, ("xh", "xl"), pairs)


def ranks(dest):
    ids = jnp.arange(dest.shape[0], dtype=jnp.int32)
    before = (ids[None, :] < ids[:, None]) & (dest[None, :] == dest[:, None])
    return jnp.sum(before.astype(jnp.int32), axis=1)


def table(dest, xh, z, c):
    ids = jnp.arange(dest.shape[0], dtype=jnp.int32)
    eight = jnp.arange(8, dtype=jnp.int32)
    cr, xr, slot = eight // 4, (eight // 2) % 2, eight % 2
    rank = ranks(dest)
    holders = ((xh ^ xr) * NZ + z) * 2 + (c ^ cr)
    in_ring = (ids // (2 * NZ) == xh) & (ids % 2 == c)
    match = (dest[None, :] == holders[:, None]) & (rank[None, :] == slot[:, None]) & in_ring[None, :]
    distance = (z - ids // 2) % NZ
    route = jnp.sum(jnp.where(match, distance[None, :] + 1, 0), axis=1) - 1
    roots = (xh * NZ + eight) * 2 + c
    root = roots[:, None] == ids[None, :]
    h = jnp.sum(jnp.where(root, dest[None], 0), axis=1)
    r = jnp.sum(jnp.where(root, rank[None], 0), axis=1)
    place = ((h % 2) ^ c) * 4 + ((h // (2 * NZ)) ^ xh) * 2 + r
    back = jnp.where((h // 2) % NZ == z, place, -1)
    mine = eight == z
    pick = jnp.sum(jnp.where(mine, (h // 2) % NZ, 0))
    return jnp.concatenate([route, back, pick[None]]).astype(jnp.int32)


def old_row(n):
    return (n // 32) % 2 * HEADS + n % 32 * 2 + n // HEADS


def pack_kernel(lat, rot, out):
    shape = (ROWS, ROWS)
    new, old = (lax.broadcasted_iota(jnp.int32, shape, d) for d in (0, 1))
    order = jnp.where(old == old_row(new), 1.0, 0.0).astype(BF)
    rows = jnp.dot(order, lat[...], preferred_element_type=F32).astype(BF)
    for j in range(COLS):
        out[j * ROWS : (j + 1) * ROWS] = rows[:, j * WIDE : (j + 1) * WIDE]
    flat = rot[...].astype(F32)
    pairs = [
        flat[s : s + 1, j * WIDE : (j + 1) * WIDE] for s in range(2) for j in range(HEADS // 2)
    ]
    out[LAT_ROWS:] = jnp.concatenate(pairs, axis=0).astype(BF)


def relay_kernel(one_up, two_up, one_down, two_down, up, down):
    up[:Q_ROWS] = one_up[...]
    up[Q_ROWS:] = two_up[:HALF]
    down[:Q_ROWS] = one_down[...]
    down[Q_ROWS:] = two_down[HALF:]


def route_kernel(t, own, one_up, two_up, one_down, two_down, up, down, keep, send):
    whole = [own, one_up, two_up, up.at[:Q_ROWS], None, down.at[:Q_ROWS], two_down, one_down]
    for slot in range(8):
        out = (keep if slot < 4 else send).at[slot % 4]
        source = t[T_ROUTE + slot]
        for d in range(NZ):

            @pl.when(source == d)
            def _():
                if d == NZ // 2:
                    out[:HALF] = up[Q_ROWS:]
                    out[HALF:] = down[Q_ROWS:]
                else:
                    out[...] = whole[d][...]

        @pl.when(source < 0)
        def _():
            out[...] = jnp.zeros(out.shape, BF)


def merge_c_kernel(keep, got, near, far):
    for r in range(2):
        near[r] = keep[r] + got[r]
        far[r] = keep[2 + r] + got[2 + r]


def merge_x_kernel(near, from_xl, from_xh, from_both, out):
    for r in range(2):
        out[r] = near[r] + from_xh[r]
        out[2 + r] = from_xl[r] + from_both[r]


def queries_of(units):
    lat, rot = [], []
    lanes = lax.broadcasted_iota(jnp.int32, (HEADS, WIDE), 1)
    for u in units:
        lat.append(jnp.concatenate([u[ROWS * j : ROWS * (j + 1)] for j in range(COLS)], axis=1))
        pair = u[LAT_ROWS:]
        zero = jnp.zeros_like(pair)
        rot += [jnp.where(lanes < ROPE, pair, zero), jnp.where(lanes < ROPE, zero, pair)]
    return jnp.concatenate(lat, axis=0), jnp.concatenate(rot, axis=0)


def prefix_kernel(q, keys, rope, o, rope2):
    rope2[:ROPE] = rope[...]
    rope2[ROPE:] = rope[...]
    for first in (0, 2):
        lat, rot = queries_of([q[first], q[first + 1]])
        s = lax.dot_general(lat, keys[...], NT, preferred_element_type=F32)
        s = s + jnp.dot(rot, rope2[...], preferred_element_type=F32)
        top = jnp.max(s, axis=1, keepdims=True)
        w = jnp.exp2((s - top) * (SCALE * LOG2E))
        total = jnp.sum(w, axis=1, keepdims=True)
        out = jnp.dot(w.astype(BF), keys[...], preferred_element_type=F32)
        out = (out / total).astype(BF)
        lse = top * SCALE + jnp.log(total)
        flat = jnp.transpose(jnp.broadcast_to(lse, (2 * ROWS, WIDE)))
        for u in range(2):
            for j in range(COLS):
                o[first + u, j * ROWS : (j + 1) * ROWS] = out[
                    u * ROWS : (u + 1) * ROWS, j * WIDE : (j + 1) * WIDE
                ]
            o[first + u, LAT_ROWS:] = in_thirds(flat[0:1, u * ROWS : (u + 1) * ROWS])


def in_thirds(row):
    high = row.astype(BF).astype(F32)
    mid = (row - high).astype(BF).astype(F32)
    low = row - high - mid
    place = lax.broadcasted_iota(jnp.int32, (16, WIDE), 0)
    block = jnp.where(place == 0, high, jnp.where(place == 1, mid, jnp.where(place == 2, low, 0.0)))
    return block.astype(BF)


def from_thirds(block):
    block = block.astype(F32)
    return block[0:1] + block[1:2] + block[2:3]


def down(row):
    return jnp.transpose(jnp.broadcast_to(row, (WIDE, WIDE)))


def merge_parts(parts, out):
    lses = [from_thirds(p[LAT_ROWS:]) for p in parts]
    top = functools.reduce(jnp.maximum, lses)
    shares = [jnp.exp(x - top) for x in lses]
    total = functools.reduce(jnp.add, shares)
    weights = [down(x / total) for x in shares]
    for j in range(COLS):
        at = slice(j * ROWS, (j + 1) * ROWS)
        mixed = [w * p[at].astype(F32) for w, p in zip(weights, parts)]
        out[at] = functools.reduce(jnp.add, mixed).astype(BF)
    out[LAT_ROWS:] = in_thirds(top + jnp.log(total))


def merge_y_kernel(p0, p1, p2, p3, near, far):
    for k in range(4):
        merge_parts([p.at[k] for p in (p0, p1, p2, p3)], (far if k // 2 else near).at[k % 2])


def merge_xl_kernel(near, from_xl, from_xh, from_both, out):
    for r in range(2):
        merge_parts([near.at[r], from_xl.at[r]], out.at[r])
        merge_parts([from_xh.at[r], from_both.at[r]], out.at[2 + r])


def back_kernel(t, own, got, out):
    for d in range(NZ):
        place = t[T_BACK + d]

        @pl.when((place >= 0) & (place < 4))
        def _():
            out[d] = own[place]

        @pl.when(place >= 4)
        def _():
            out[d] = got[place - 4]

        @pl.when(place < 0)
        def _():
            out[d] = jnp.zeros((OUT_ROWS, WIDE), BF)


def suffix_kernel(length, unit, keys, rope, out, out_lse, rope2):
    rope2[:ROPE] = rope[...]
    rope2[ROPE:] = rope[...]
    lat, rot = queries_of([unit[...]])
    s = lax.dot_general(lat, keys[...], NT, preferred_element_type=F32)
    s = (s + jnp.dot(rot, rope2[...], preferred_element_type=F32)) * SCALE
    position = lax.broadcasted_iota(jnp.int32, s.shape, 1)
    step = lax.broadcasted_iota(jnp.int32, s.shape, 0) // (HEADS // 2) % 2
    s = jnp.where(position < length[0] + step + 1, s, -1e30)
    top = jnp.max(s, axis=1, keepdims=True)
    w = jnp.exp(s - top)
    total = jnp.sum(w, axis=1, keepdims=True)
    out[...] = jnp.dot(w.astype(BF), keys[...], preferred_element_type=F32) / total
    out_lse[...] = jnp.broadcast_to(top + jnp.log(total), out_lse.shape)


def final_kernel(t, units, suffix, suf, out):
    held = units.at[t[T_PICK]]
    pre = down(from_thirds(held[LAT_ROWS:]))
    top = jnp.maximum(pre, suf[...])
    w_pre, w_suf = jnp.exp(pre - top), jnp.exp(suf[...] - top)
    total = w_pre + w_suf
    shape = (ROWS, ROWS)
    old, new = (lax.broadcasted_iota(jnp.int32, shape, d) for d in (0, 1))
    order = jnp.where(old == old_row(new), 1.0, 0.0).astype(BF)
    for j in range(COLS):
        got = held[j * ROWS : (j + 1) * ROWS].astype(F32)
        cols = slice(j * WIDE, (j + 1) * WIDE)
        mixed = ((w_pre * got + w_suf * suffix[:, cols]) / total).astype(BF)
        out[:, cols] = jnp.dot(order, mixed, preferred_element_type=F32).astype(BF)


def body(
    q_latent, q_rope, prefix_latent, prefix_rope, suffix_latent, suffix_rope, prefix_of, suffix_len
):
    rows, latent = q_latent.shape[1] * q_latent.shape[2], q_latent.shape[3]
    xh, z, c = (lax.axis_index(a) for a in ("xh", "z", "c"))
    unit = shaped(Q_ROWS, WIDE)
    own = call(pack_kernel, unit, [], [q_latent[0].reshape(rows, latent), q_rope[0]])

    one_up, one_down = along(own, "z", 1), along(own, "z", -1)
    two_up, two_down = along(own, "z", 2), along(own, "z", -2)
    more = shaped(Q_ROWS + HALF, WIDE)
    up, down_ = call(
        relay_kernel, [more, more], [], [one_up, two_up, one_down, two_down], bytes_accessed=1 << 20
    )
    up, down_ = along(up, "z", 2), along(down_, "z", -2)

    t = table(prefix_of[0, :, 0], xh, z, c)
    keys, rope = prefix_latent[0], prefix_rope[0]
    positions = keys.shape[0]
    attend = functools.partial(
        pl.pallas_call,
        scratch_shapes=[pltpu.VMEM((2 * ROPE, positions), BF)],
        compiler_params=pltpu.CompilerParams(vmem_limit_bytes=48 * 1024 * 1024),
    )
    suffix, suffix_lse = attend(
        suffix_kernel,
        out_shape=[shaped(rows, LATENT, dtype=F32), shaped(rows, WIDE, dtype=F32)],
        in_specs=[SMEM, VMEM, VMEM, VMEM],
        out_specs=[VMEM, VMEM],
        cost_estimate=pl.CostEstimate(
            flops=2 * rows * 2048 * 1152, bytes_accessed=3 << 20, transcendentals=rows * 2048
        ),
    )(suffix_len, own, suffix_latent[0], suffix_rope[0])

    quad, two = shaped(4, Q_ROWS, WIDE), shaped(2, Q_ROWS, WIDE)
    keep, send = call(
        route_kernel,
        [quad, quad],
        [t],
        [own, one_up, two_up, one_down, two_down, up, down_],
        bytes_accessed=1 << 20,
    )
    near, far = call(
        merge_c_kernel, [two, two], [], [keep, along(send, "c", 1)], bytes_accessed=1 << 20
    )
    mine = call(
        merge_x_kernel,
        quad,
        [],
        [near, across(near, 0, 1), across(far, 1, 0), across(far, 1, 1)],
        bytes_accessed=1 << 20,
    )
    asked = {d: along(mine, "y", d) if d else mine for d in (0, 1, 3, 2)}

    outs = shaped(4, OUT_ROWS, WIDE)
    parts = {}
    for d, queries in asked.items():
        if d == 1:
            queries, parts[0] = lax.optimization_barrier((queries, parts[0]))
        part = attend(
            prefix_kernel,
            out_shape=outs,
            in_specs=[VMEM] * 3,
            out_specs=VMEM,
            cost_estimate=pl.CostEstimate(
                flops=2 * 512 * 2048 * 1152, bytes_accessed=4 << 20, transcendentals=512 * 2048
            ),
        )(queries, keys, rope)
        parts[d] = along(part, "y", -d) if d else part
    out2 = shaped(2, OUT_ROWS, WIDE)
    p_near, p_far = call(
        merge_y_kernel, [out2, out2], [], [parts[d] for d in range(NY)], bytes_accessed=1 << 20
    )
    both = call(
        merge_xl_kernel,
        outs,
        [],
        [p_near, across(p_far, 0, 1), across(p_near, 1, 0), across(p_far, 1, 1)],
        bytes_accessed=1 << 20,
    )
    back = call(
        back_kernel,
        shaped(NZ, OUT_ROWS, WIDE),
        [t],
        [both, along(both, "c", 1)],
        bytes_accessed=1 << 20,
    )
    arrived = lax.all_to_all(back, "z", 0, 0, tiled=True)
    out = call(
        final_kernel,
        shaped(rows, LATENT),
        [t],
        [arrived, suffix, suffix_lse],
        bytes_accessed=1 << 20,
    )
    return out.reshape(q_latent.shape)


def solution(mesh):
    fine = Mesh(mesh.devices.reshape(2, NZ, 2, NY, 2), AXES)
    grp, blk = ("xh", "z", "c"), ("y", "xl")
    in_specs = (
        P(AXES, None, None, None),
        P(AXES, None, None),
        P(grp, blk, None),
        P(grp, None, blk),
        P(AXES, None, None),
        P(AXES, None, None),
        P(blk, None, None),
        P(AXES),
    )
    return jax.shard_map(
        body, mesh=fine, in_specs=in_specs, out_specs=P(AXES, None, None, None), check_vma=False
    )
```

time: 205 us -> 174 us (0.85)
  the two profiles are of different devices: /device:TPU:8 before, /device:TPU:1 now
where the time goes in v1:
time: 174 us
  waiting for transfers between devices  107 us (61%)
  starting transfers between devices  37.5 us (22%)
  Pallas kernels  20.9 us (12%)
  local copies, waits for them, and re-layouts  4.22 us (2%)
  other arithmetic  3.19 us (2%)
    ppermute x14, waiting for transfers between devices, along(): return lax.ppermute(x, axis, [(i, (i + distance) % n) for i in range(n)])  54.7 us
    ppermute x6, waiting for transfers between devices, across(): return lax.ppermute(x, ('xh', 'xl'), pairs)  26.1 us
    all_to_all x1, waiting for transfers between devices, body(): arrived = lax.all_to_all(back, 'z', 0, 0, tiled=True)  26 us
    ppermute x14, starting transfers between devices, along(): return lax.ppermute(x, axis, [(i, (i + distance) % n) for i in range(n)])  24.3 us
    pallas_call x4, Pallas kernels, body(): attend(prefix_kernel, out_shape=outs, in_specs=[VMEM] * 3, out_specs=VMEM...  13.8 us
    ppermute x6, starting transfers between devices, across(): return lax.ppermute(x, ('xh', 'xl'), pairs)  7.88 us
    pallas_call x9, Pallas kernels, call(): pl.pallas_call(kernel, out_shape=outs, in_specs=[SMEM] * len(ints) + [VME...  5.53 us
    all_to_all x1, starting transfers between devices, body(): arrived = lax.all_to_all(back, 'z', 0, 0, tiled=True)  5.37 us
  transfers between devices with their start and end apart: 21, of which 18 were waited for; matrix products, arithmetic and copies ran while one was open for 2% of the time, Pallas kernels for 9%

profile of v1, /device:TPU:1, one launch (start us, length us, event | category | flops | bytes accessed | tf_op | source)
XLA Modules:
  0.0 173.5 jit_solution(13438843530878732692)
XLA Ops:
  0.0 0.9 copy-done.4
  1.8 2.5 %collective-permute-start = (bf16[576,128]{1,0:T(8,128)(2,1)S(1)}, bf16[576,128]{1,0:T(8,128)(2,1)S(1)}, u32[]{:S(2)}, u32[]{:S(2)}) collective-permute-start(bf16[576,128]{1,0:T(8,128)(2,1)S(1)} %shard_map.82.own.unit), channel_id=1, source_target_pairs={{0,16},{16,32},{32,48},{48,64},{64,80},{80,96},{96,112},{112,0},{1... | collective-permute-start | bytes 442376 | tf_op jit(solution)/shard_map/ppermute | solution.py:55
  4.3 3.0 %collective-permute-start.1 = (bf16[576,128]{1,0:T(8,128)(2,1)S(1)}, bf16[576,128]{1,0:T(8,128)(2,1)S(1)}, u32[]{:S(2)}, u32[]{:S(2)}) collective-permute-start(bf16[576,128]{1,0:T(8,128)(2,1)S(1)} %shard_map.82.own.unit), channel_id=1, source_target_pairs={{0,32},{16,48},{32,64},{48,80},{64,96},{80,112},{96,0},{112,16},{1... | collective-permute-start | bytes 442376 | tf_op jit(solution)/shard_map/ppermute | solution.py:55
  7.3 1.1 collective-permute-start.2
  8.5 2.3 %collective-permute-start.3 = (bf16[576,128]{1,0:T(8,128)(2,1)S(1)}, bf16[576,128]{1,0:T(8,128)(2,1)S(1)}, u32[]{:S(2)}, u32[]{:S(2)}) collective-permute-start(bf16[576,128]{1,0:T(8,128)(2,1)S(1)} %shard_map.82.own.unit), channel_id=1, source_target_pairs={{0,96},{16,112},{32,0},{48,16},{64,32},{80,48},{96,64},{112,80},{1... | collective-permute-start | bytes 442376 | tf_op jit(solution)/shard_map/ppermute | solution.py:55
  10.8 0.9 convert_reduce_fusion
  11.7 0.9 select_reduce_fusion.2
  12.6 4.1 %collective-permute-done.1.two_up = bf16[576,128]{1,0:T(8,128)(2,1)S(1)} collective-permute-done((bf16[576,128]{1,0:T(8,128)(2,1)S(1)}, bf16[576,128]{1,0:T(8,128)(2,1)S(1)}, u32[]{:S(2)}, u32[]{:S(2)}) %collective-permute-start.1) | collective-permute-done | bytes 147488 | tf_op jit(solution)/shard_map/ppermute | solution.py:55
  16.7 2.3 %collective-permute-done.3.two_down = bf16[576,128]{1,0:T(8,128)(2,1)S(1)} collective-permute-done((bf16[576,128]{1,0:T(8,128)(2,1)S(1)}, bf16[576,128]{1,0:T(8,128)(2,1)S(1)}, u32[]{:S(2)}, u32[]{:S(2)}) %collective-permute-start.3) | collective-permute-done | bytes 147488 | tf_op jit(solution)/shard_map/ppermute | solution.py:55
  19.1 2.5 %collective-permute-start.4 = (bf16[864,128]{1,0:T(8,128)(2,1)S(1)}, bf16[864,128]{1,0:T(8,128)(2,1)S(1)}, u32[]{:S(2)}, u32[]{:S(2)}) collective-permute-start(bf16[864,128]{1,0:T(8,128)(2,1)S(1)} %get-tuple-element.17), channel_id=1, source_target_pairs={{0,32},{16,48},{32,64},{48,80},{64,96},{80,112},{96,0},{112,16},{1... | collective-permute-start | bytes 663560 | tf_op jit(solution)/shard_map/ppermute | solution.py:55
  21.6 1.1 collective-permute-start.5
  24.1 2.4 %collective-permute-done.4.up = bf16[864,128]{1,0:T(8,128)(2,1)S(1)} collective-permute-done((bf16[864,128]{1,0:T(8,128)(2,1)S(1)}, bf16[864,128]{1,0:T(8,128)(2,1)S(1)}, u32[]{:S(2)}, u32[]{:S(2)}) %collective-permute-start.4) | collective-permute-done | bytes 221216 | tf_op jit(solution)/shard_map/ppermute | solution.py:55
  26.5 6.7 %collective-permute-done.5.down = bf16[864,128]{1,0:T(8,128)(2,1)S(1)} collective-permute-done((bf16[864,128]{1,0:T(8,128)(2,1)S(1)}, bf16[864,128]{1,0:T(8,128)(2,1)S(1)}, u32[]{:S(2)}, u32[]{:S(2)}) %collective-permute-start.5) | collective-permute-done | bytes 221216 | tf_op jit(solution)/shard_map/ppermute | solution.py:55
  33.2 1.0 shard_map.84
  34.2 2.0 %collective-permute-start.6 = (bf16[4,576,128]{2,1,0:T(8,128)(2,1)S(1)}, bf16[4,576,128]{2,1,0:T(8,128)(2,1)S(1)}, u32[]{:S(2)}, u32[]{:S(2)}) collective-permute-start(bf16[4,576,128]{2,1,0:T(8,128)(2,1)S(1)} %get-tuple-element.20), channel_id=1, source_target_pairs={{0,8},{8,0},{1,9},{9,1},{2,10},{10,2},{3,11},{11,3},{4,12},{12,4},... | collective-permute-start | bytes 1769480 | tf_op jit(solution)/shard_map/ppermute | solution.py:55
  36.2 1.6 collective-permute-done.6.got
  38.0 1.3 collective-permute-start.7
  39.3 2.5 %collective-permute-start.8 = (bf16[2,576,128]{2,1,0:T(8,128)(2,1)S(1)}, bf16[2,576,128]{2,1,0:T(8,128)(2,1)S(1)}, u32[]{:S(2)}, u32[]{:S(2)}) collective-permute-start(bf16[2,576,128]{2,1,0:T(8,128)(2,1)S(1)} %get-tuple-element.22), channel_id=1, source_target_pairs={{0,128},{1,129},{128,0},{129,1},{2,130},{3,131},{130,2},{131,3},{4... | collective-permute-start | bytes 884744 | tf_op jit(solution)/shard_map/ppermute | solution.py:62
  41.9 4.4 %collective-permute-done.7.from_xl = bf16[2,576,128]{2,1,0:T(8,128)(2,1)S(1)} collective-permute-done((bf16[2,576,128]{2,1,0:T(8,128)(2,1)S(1)}, bf16[2,576,128]{2,1,0:T(8,128)(2,1)S(1)}, u32[]{:S(2)}, u32[]{:S(2)}) %collective-permute-start.7) | collective-permute-done | bytes 294944 | tf_op jit(solution)/shard_map/ppermute | solution.py:62
  46.3 8.6 %collective-permute-done.8.from_xh = bf16[2,576,128]{2,1,0:T(8,128)(2,1)S(1)} collective-permute-done((bf16[2,576,128]{2,1,0:T(8,128)(2,1)S(1)}, bf16[2,576,128]{2,1,0:T(8,128)(2,1)S(1)}, u32[]{:S(2)}, u32[]{:S(2)}) %collective-permute-start.8) | collective-permute-done | bytes 294944 | tf_op jit(solution)/shard_map/ppermute | solution.py:62
  54.8 2.0 %collective-permute-done.9.from_both = bf16[2,576,128]{2,1,0:T(8,128)(2,1)S(1)} collective-permute-done((bf16[2,576,128]{2,1,0:T(8,128)(2,1)S(1)}, bf16[2,576,128]{2,1,0:T(8,128)(2,1)S(1)}, u32[]{:S(2)}, u32[]{:S(2)}) %collective-permute-start.9) | collective-permute-done | bytes 294944 | tf_op jit(solution)/shard_map/ppermute | solution.py:62
  56.9 1.4 collective-permute-start.10
  58.3 2.6 %collective-permute-start.12 = (bf16[4,576,128]{2,1,0:T(8,128)(2,1)S(1)}, bf16[4,576,128]{2,1,0:T(8,128)(2,1)S(1)}, u32[]{:S(2)}, u32[]{:S(2)}) collective-permute-start(bf16[4,576,128]{2,1,0:T(8,128)(2,1)S(1)} %shard_map.86.q), channel_id=1, source_target_pairs={{0,4},{2,6},{4,0},{6,2},{1,5},{3,7},{5,1},{7,3},{8,12},{10,14},{12... | collective-permute-start | bytes 1769480 | tf_op jit(solution)/shard_map/ppermute | solution.py:55
  61.0 1.1 collective-permute-start.14
  62.0 3.5 %shard_map.87.p0 = bf16[4,528,128]{2,1,0:T(8,128)(2,1)S(1)} custom-call(bf16[4,576,128]{2,1,0:T(8,128)(2,1)S(1)} %shard_map.86.q, bf16[2048,512]{1,0:T(8,128)(2,1)S(1)} %bitcast.13, bf16[64,2048]{1,0:T(8,128)(2,1)S(1)} %bitcast.17), custom_call_target="tpu_custom_call" | custom-call | flops 2415919104 | bytes 4194304 | tf_op jit(solution)/shard_map/pallas_call | solution.py:332
  65.5 5.8 %collective-permute-done.10.q = bf16[4,576,128]{2,1,0:T(8,128)(2,1)S(1)} collective-permute-done((bf16[4,576,128]{2,1,0:T(8,128)(2,1)S(1)}, bf16[4,576,128]{2,1,0:T(8,128)(2,1)S(1)}, u32[]{:S(2)}, u32[]{:S(2)}) %collective-permute-start.10) | collective-permute-done | bytes 589856 | tf_op jit(solution)/shard_map/ppermute | solution.py:55
  71.4 3.5 %shard_map.88 = bf16[4,528,128]{2,1,0:T(8,128)(2,1)S(1)} custom-call(bf16[4,576,128]{2,1,0:T(8,128)(2,1)S(1)} %collective-permute-done.10.q, bf16[2048,512]{1,0:T(8,128)(2,1)S(1)} %bitcast.14, bf16[64,2048]{1,0:T(8,128)(2,1)S(1)} %bitcast.18), custom_call_target="tpu_custom_call" | custom-call | flops 2415919104 | bytes 4194304 | tf_op jit(solution)/shard_map/pallas_call | solution.py:332
  74.8 1.5 collective-permute-start.11
  76.3 8.8 %collective-permute-done.12.q = bf16[4,576,128]{2,1,0:T(8,128)(2,1)S(1)} collective-permute-done((bf16[4,576,128]{2,1,0:T(8,128)(2,1)S(1)}, bf16[4,576,128]{2,1,0:T(8,128)(2,1)S(1)}, u32[]{:S(2)}, u32[]{:S(2)}) %collective-permute-start.12) | collective-permute-done | bytes 589856 | tf_op jit(solution)/shard_map/ppermute | solution.py:55
  85.1 3.5 %shard_map.89 = bf16[4,528,128]{2,1,0:T(8,128)(2,1)S(1)} custom-call(bf16[4,576,128]{2,1,0:T(8,128)(2,1)S(1)} %collective-permute-done.12.q, bf16[2048,512]{1,0:T(8,128)(2,1)S(1)} %bitcast.15, bf16[64,2048]{1,0:T(8,128)(2,1)S(1)} %bitcast.19), custom_call_target="tpu_custom_call" | custom-call | flops 2415919104 | bytes 4194304 | tf_op jit(solution)/shard_map/pallas_call | solution.py:332
  89.1 3.5 %shard_map.90 = bf16[4,528,128]{2,1,0:T(8,128)(2,1)S(1)} custom-call(bf16[4,576,128]{2,1,0:T(8,128)(2,1)S(1)} %collective-permute-done.14.q, bf16[2048,512]{1,0:T(8,128)(2,1)S(1)} %bitcast.16, bf16[64,2048]{1,0:T(8,128)(2,1)S(1)} %bitcast.20), custom_call_target="tpu_custom_call" | custom-call | flops 2415919104 | bytes 4194304 | tf_op jit(solution)/shard_map/pallas_call | solution.py:332
  92.8 6.5 %collective-permute-done.11.p1 = bf16[4,528,128]{2,1,0:T(8,128)(2,1)S(1)} collective-permute-done((bf16[4,528,128]{2,1,0:T(8,128)(2,1)S(1)}, bf16[4,528,128]{2,1,0:T(8,128)(2,1)S(1)}, u32[]{:S(2)}, u32[]{:S(2)}) %collective-permute-start.11) | collective-permute-done | bytes 540704 | tf_op jit(solution)/shard_map/ppermute | solution.py:55
  99.3 1.1 collective-permute-done.13.p2
  100.4 13.8 %collective-permute-done.15.p3 = bf16[4,528,128]{2,1,0:T(8,128)(2,1)S(1)} collective-permute-done((bf16[4,528,128]{2,1,0:T(8,128)(2,1)S(1)}, bf16[4,528,128]{2,1,0:T(8,128)(2,1)S(1)}, u32[]{:S(2)}, u32[]{:S(2)}) %collective-permute-start.15) | collective-permute-done | bytes 540704 | tf_op jit(solution)/shard_map/ppermute | solution.py:55
  114.8 1.4 collective-permute-start.17
  116.2 2.5 %collective-permute-start.18 = (bf16[2,528,128]{2,1,0:T(8,128)(2,1)S(1)}, bf16[2,528,128]{2,1,0:T(8,128)(2,1)S(1)}, u32[]{:S(2)}, u32[]{:S(2)}) collective-permute-start(bf16[2,528,128]{2,1,0:T(8,128)(2,1)S(1)} %get-tuple-element.26), channel_id=1, source_target_pairs={{0,129},{1,128},{128,1},{129,0},{2,131},{3,130},{130,3},{131,2},{4... | collective-permute-start | bytes 811016 | tf_op jit(solution)/shard_map/ppermute | solution.py:62
  118.6 1.9 %collective-permute-done.16.from_xl = bf16[2,528,128]{2,1,0:T(8,128)(2,1)S(1)} collective-permute-done((bf16[2,528,128]{2,1,0:T(8,128)(2,1)S(1)}, bf16[2,528,128]{2,1,0:T(8,128)(2,1)S(1)}, u32[]{:S(2)}, u32[]{:S(2)}) %collective-permute-start.16) | collective-permute-done | bytes 270368 | tf_op jit(solution)/shard_map/ppermute | solution.py:62
  120.5 5.7 %collective-permute-done.17.from_xh = bf16[2,528,128]{2,1,0:T(8,128)(2,1)S(1)} collective-permute-done((bf16[2,528,128]{2,1,0:T(8,128)(2,1)S(1)}, bf16[2,528,128]{2,1,0:T(8,128)(2,1)S(1)}, u32[]{:S(2)}, u32[]{:S(2)}) %collective-permute-start.17) | collective-permute-done | bytes 270368 | tf_op jit(solution)/shard_map/ppermute | solution.py:62
  126.2 3.6 %collective-permute-done.18.from_both = bf16[2,528,128]{2,1,0:T(8,128)(2,1)S(1)} collective-permute-done((bf16[2,528,128]{2,1,0:T(8,128)(2,1)S(1)}, bf16[2,528,128]{2,1,0:T(8,128)(2,1)S(1)}, u32[]{:S(2)}, u32[]{:S(2)}) %collective-permute-start.18) | collective-permute-done | bytes 270368 | tf_op jit(solution)/shard_map/ppermute | solution.py:62
  130.1 2.4 %collective-permute-start.19 = (bf16[4,528,128]{2,1,0:T(8,128)(2,1)S(1)}, bf16[4,528,128]{2,1,0:T(8,128)(2,1)S(1)}, u32[]{:S(2)}, u32[]{:S(2)}) collective-permute-start(bf16[4,528,128]{2,1,0:T(8,128)(2,1)S(1)} %shard_map.92.own), channel_id=1, source_target_pairs={{0,8},{8,0},{1,9},{9,1},{2,10},{10,2},{3,11},{11,3},{4,12},{12,4},... | collective-permute-start | bytes 1622024 | tf_op jit(solution)/shard_map/ppermute | solution.py:55
  132.4 1.6 collective-permute-done.19.got
  134.0 1.8 %shard_map.93 = bf16[8,528,128]{2,1,0:T(8,128)(2,1)} custom-call(s32[17]{0:T(128)S(1)} %pad_add_fusion.t, bf16[4,528,128]{2,1,0:T(8,128)(2,1)S(1)} %shard_map.92.own, bf16[4,528,128]{2,1,0:T(8,128)(2,1)S(1)} %collective-permute-done.19.got), custom_call_target="tpu_custom_call" | custom-call | bytes 1048576 | tf_op jit(solution)/shard_map/pallas_call | solution.py:37
  135.8 5.4 %all-to-all-start = ((bf16[8,528,128]{2,1,0:T(8,128)(2,1)}), bf16[8,528,128]{2,1,0:T(8,128)(2,1)S(1)}, u32[]{:S(2)}, u32[]{:S(2)}) async-start(bf16[8,528,128]{2,1,0:T(8,128)(2,1)} %shard_map.93), calls=%async_computation | async-start | bytes 2162688 | tf_op jit(solution)/shard_map/all_to_all | solution.py:360
  141.8 0.9 copy-done.3
  142.8 1.6 shard_map.94
  145.1 26.0 %all-to-all-done.units = bf16[8,528,128]{2,1,0:T(8,128)(2,1)S(1)} async-done(((bf16[8,528,128]{2,1,0:T(8,128)(2,1)}), bf16[8,528,128]{2,1,0:T(8,128)(2,1)S(1)}, u32[]{:S(2)}, u32[]{:S(2)}) %all-to-all-start) | async-done | bytes 1081376 | tf_op jit(solution)/shard_map/all_to_all | solution.py:360
  171.1 0.9 copy-done.2
  172.1 1.5 shard_map.95
  (34 shorter events, 5.2 us)
Async XLA Ops:
  0.0 0.9 copy-start.4
  0.9 0.7 copy-start.5
  1.8 10.8 %collective-permute-start = (bf16[576,128]{1,0:T(8,128)(2,1)S(1)}, bf16[576,128]{1,0:T(8,128)(2,1)S(1)}, u32[]{:S(2)}, u32[]{:S(2)}) collective-permute-start(bf16[576,128]{1,0:T(8,128)(2,1)S(1)} %shard_map.82.own.unit), channel_id=1, source_target_pairs={{0,16},{16,32},{32,48},{48,64},{64,80},{80,96},{96,112},{112,0},{1... | collective-permute-start | bytes 442376 | tf_op jit(solution)/shard_map/ppermute | solution.py:55
  4.3 12.4 %collective-permute-start.1 = (bf16[576,128]{1,0:T(8,128)(2,1)S(1)}, bf16[576,128]{1,0:T(8,128)(2,1)S(1)}, u32[]{:S(2)}, u32[]{:S(2)}) collective-permute-start(bf16[576,128]{1,0:T(8,128)(2,1)S(1)} %shard_map.82.own.unit), channel_id=1, source_target_pairs={{0,32},{16,48},{32,64},{48,80},{64,96},{80,112},{96,0},{112,16},{1... | collective-permute-start | bytes 442376 | tf_op jit(solution)/shard_map/ppermute | solution.py:55
  7.3 9.4 %collective-permute-start.2 = (bf16[576,128]{1,0:T(8,128)(2,1)S(1)}, bf16[576,128]{1,0:T(8,128)(2,1)S(1)}, u32[]{:S(2)}, u32[]{:S(2)}) collective-permute-start(bf16[576,128]{1,0:T(8,128)(2,1)S(1)} %shard_map.82.own.unit), channel_id=1, source_target_pairs={{0,112},{16,0},{32,16},{48,32},{64,48},{80,64},{96,80},{112,96},{1... | collective-permute-start | bytes 442376 | tf_op jit(solution)/shard_map/ppermute | solution.py:55
  8.5 10.6 %collective-permute-start.3 = (bf16[576,128]{1,0:T(8,128)(2,1)S(1)}, bf16[576,128]{1,0:T(8,128)(2,1)S(1)}, u32[]{:S(2)}, u32[]{:S(2)}) collective-permute-start(bf16[576,128]{1,0:T(8,128)(2,1)S(1)} %shard_map.82.own.unit), channel_id=1, source_target_pairs={{0,96},{16,112},{32,0},{48,16},{64,32},{80,48},{96,64},{112,80},{1... | collective-permute-start | bytes 442376 | tf_op jit(solution)/shard_map/ppermute | solution.py:55
  19.1 43.0 %copy-start.6 = (bf16[1,2048,512]{2,1,0:T(8,128)(2,1)S(1)}, bf16[1,2048,512]{2,1,0:T(8,128)(2,1)}, u32[]{:S(2)}) copy-start(bf16[1,2048,512]{2,1,0:T(8,128)(2,1)} %param.10) | copy-start | bytes 6291460
  19.1 43.0 %copy-start.7 = (bf16[1,64,2048]{2,1,0:T(8,128)(2,1)S(1)}, bf16[1,64,2048]{2,1,0:T(8,128)(2,1)}, u32[]{:S(2)}) copy-start(bf16[1,64,2048]{2,1,0:T(8,128)(2,1)} %param.11) | copy-start | bytes 786436
  19.1 7.4 %collective-permute-start.4 = (bf16[864,128]{1,0:T(8,128)(2,1)S(1)}, bf16[864,128]{1,0:T(8,128)(2,1)S(1)}, u32[]{:S(2)}, u32[]{:S(2)}) collective-permute-start(bf16[864,128]{1,0:T(8,128)(2,1)S(1)} %get-tuple-element.17), channel_id=1, source_target_pairs={{0,32},{16,48},{32,64},{48,80},{64,96},{80,112},{96,0},{112,16},{1... | collective-permute-start | bytes 663560 | tf_op jit(solution)/shard_map/ppermute | solution.py:55
  21.6 11.6 %collective-permute-start.5 = (bf16[864,128]{1,0:T(8,128)(2,1)S(1)}, bf16[864,128]{1,0:T(8,128)(2,1)S(1)}, u32[]{:S(2)}, u32[]{:S(2)}) collective-permute-start(bf16[864,128]{1,0:T(8,128)(2,1)S(1)} %get-tuple-element.18), channel_id=1, source_target_pairs={{0,96},{16,112},{32,0},{48,16},{64,32},{80,48},{96,64},{112,80},{1... | collective-permute-start | bytes 663560 | tf_op jit(solution)/shard_map/ppermute | solution.py:55
  34.2 3.6 %collective-permute-start.6 = (bf16[4,576,128]{2,1,0:T(8,128)(2,1)S(1)}, bf16[4,576,128]{2,1,0:T(8,128)(2,1)S(1)}, u32[]{:S(2)}, u32[]{:S(2)}) collective-permute-start(bf16[4,576,128]{2,1,0:T(8,128)(2,1)S(1)} %get-tuple-element.20), channel_id=1, source_target_pairs={{0,8},{8,0},{1,9},{9,1},{2,10},{10,2},{3,11},{11,3},{4,12},{12,4},... | collective-permute-start | bytes 1769480 | tf_op jit(solution)/shard_map/ppermute | solution.py:55
  38.0 8.3 %collective-permute-start.7 = (bf16[2,576,128]{2,1,0:T(8,128)(2,1)S(1)}, bf16[2,576,128]{2,1,0:T(8,128)(2,1)S(1)}, u32[]{:S(2)}, u32[]{:S(2)}) collective-permute-start(bf16[2,576,128]{2,1,0:T(8,128)(2,1)S(1)} %get-tuple-element.21.near), channel_id=1, source_target_pairs={{0,1},{1,0},{128,129},{129,128},{2,3},{3,2},{130,131},{131,130},{4... | collective-permute-start | bytes 884744 | tf_op jit(solution)/shard_map/ppermute | solution.py:62
  39.3 15.6 %collective-permute-start.8 = (bf16[2,576,128]{2,1,0:T(8,128)(2,1)S(1)}, bf16[2,576,128]{2,1,0:T(8,128)(2,1)S(1)}, u32[]{:S(2)}, u32[]{:S(2)}) collective-permute-start(bf16[2,576,128]{2,1,0:T(8,128)(2,1)S(1)} %get-tuple-element.22), channel_id=1, source_target_pairs={{0,128},{1,129},{128,0},{129,1},{2,130},{3,131},{130,2},{131,3},{4... | collective-permute-start | bytes 884744 | tf_op jit(solution)/shard_map/ppermute | solution.py:62
  41.7 15.1 %collective-permute-start.9 = (bf16[2,576,128]{2,1,0:T(8,128)(2,1)S(1)}, bf16[2,576,128]{2,1,0:T(8,128)(2,1)S(1)}, u32[]{:S(2)}, u32[]{:S(2)}) collective-permute-start(bf16[2,576,128]{2,1,0:T(8,128)(2,1)S(1)} %get-tuple-element.22), channel_id=1, source_target_pairs={{0,129},{1,128},{128,1},{129,0},{2,131},{3,130},{130,3},{131,2},{4... | collective-permute-start | bytes 884744 | tf_op jit(solution)/shard_map/ppermute | solution.py:62
  56.9 14.4 %collective-permute-start.10 = (bf16[4,576,128]{2,1,0:T(8,128)(2,1)S(1)}, bf16[4,576,128]{2,1,0:T(8,128)(2,1)S(1)}, u32[]{:S(2)}, u32[]{:S(2)}) collective-permute-start(bf16[4,576,128]{2,1,0:T(8,128)(2,1)S(1)} %shard_map.86.q), channel_id=1, source_target_pairs={{0,2},{2,4},{4,6},{6,0},{1,3},{3,5},{5,7},{7,1},{8,10},{10,12},{12... | collective-permute-start | bytes 1769480 | tf_op jit(solution)/shard_map/ppermute | solution.py:55
  58.3 26.8 %collective-permute-start.12 = (bf16[4,576,128]{2,1,0:T(8,128)(2,1)S(1)}, bf16[4,576,128]{2,1,0:T(8,128)(2,1)S(1)}, u32[]{:S(2)}, u32[]{:S(2)}) collective-permute-start(bf16[4,576,128]{2,1,0:T(8,128)(2,1)S(1)} %shard_map.86.q), channel_id=1, source_target_pairs={{0,4},{2,6},{4,0},{6,2},{1,5},{3,7},{5,1},{7,3},{8,12},{10,14},{12... | collective-permute-start | bytes 1769480 | tf_op jit(solution)/shard_map/ppermute | solution.py:55
  61.0 28.1 %collective-permute-start.14 = (bf16[4,576,128]{2,1,0:T(8,128)(2,1)S(1)}, bf16[4,576,128]{2,1,0:T(8,128)(2,1)S(1)}, u32[]{:S(2)}, u32[]{:S(2)}) collective-permute-start(bf16[4,576,128]{2,1,0:T(8,128)(2,1)S(1)} %shard_map.86.q), channel_id=1, source_target_pairs={{0,6},{2,0},{4,2},{6,4},{1,7},{3,1},{5,3},{7,5},{8,14},{10,8},{12,... | collective-permute-start | bytes 1769480 | tf_op jit(solution)/shard_map/ppermute | solution.py:55
  74.8 24.5 %collective-permute-start.11 = (bf16[4,528,128]{2,1,0:T(8,128)(2,1)S(1)}, bf16[4,528,128]{2,1,0:T(8,128)(2,1)S(1)}, u32[]{:S(2)}, u32[]{:S(2)}) collective-permute-start(bf16[4,528,128]{2,1,0:T(8,128)(2,1)S(1)} %shard_map.88), channel_id=1, source_target_pairs={{0,6},{2,0},{4,2},{6,4},{1,7},{3,1},{5,3},{7,5},{8,14},{10,8},{12,... | collective-permute-start | bytes 1622024 | tf_op jit(solution)/shard_map/ppermute | solution.py:55
  88.6 11.8 %collective-permute-start.13 = (bf16[4,528,128]{2,1,0:T(8,128)(2,1)S(1)}, bf16[4,528,128]{2,1,0:T(8,128)(2,1)S(1)}, u32[]{:S(2)}, u32[]{:S(2)}) collective-permute-start(bf16[4,528,128]{2,1,0:T(8,128)(2,1)S(1)} %shard_map.89), channel_id=1, source_target_pairs={{0,4},{2,6},{4,0},{6,2},{1,5},{3,7},{5,1},{7,3},{8,12},{10,14},{12... | collective-permute-start | bytes 1622024 | tf_op jit(solution)/shard_map/ppermute | solution.py:55
  92.5 21.7 %collective-permute-start.15 = (bf16[4,528,128]{2,1,0:T(8,128)(2,1)S(1)}, bf16[4,528,128]{2,1,0:T(8,128)(2,1)S(1)}, u32[]{:S(2)}, u32[]{:S(2)}) collective-permute-start(bf16[4,528,128]{2,1,0:T(8,128)(2,1)S(1)} %shard_map.90), channel_id=1, source_target_pairs={{0,2},{2,4},{4,6},{6,0},{1,3},{3,5},{5,7},{7,1},{8,10},{10,12},{12... | collective-permute-start | bytes 1622024 | tf_op jit(solution)/shard_map/ppermute | solution.py:55
  114.7 5.8 %collective-permute-start.16 = (bf16[2,528,128]{2,1,0:T(8,128)(2,1)S(1)}, bf16[2,528,128]{2,1,0:T(8,128)(2,1)S(1)}, u32[]{:S(2)}, u32[]{:S(2)}) collective-permute-start(bf16[2,528,128]{2,1,0:T(8,128)(2,1)S(1)} %get-tuple-element.26), channel_id=1, source_target_pairs={{0,1},{1,0},{128,129},{129,128},{2,3},{3,2},{130,131},{131,130},{4... | collective-permute-start | bytes 811016 | tf_op jit(solution)/shard_map/ppermute | solution.py:62
  114.8 11.4 %collective-permute-start.17 = (bf16[2,528,128]{2,1,0:T(8,128)(2,1)S(1)}, bf16[2,528,128]{2,1,0:T(8,128)(2,1)S(1)}, u32[]{:S(2)}, u32[]{:S(2)}) collective-permute-start(bf16[2,528,128]{2,1,0:T(8,128)(2,1)S(1)} %get-tuple-element.25.near), channel_id=1, source_target_pairs={{0,128},{1,129},{128,0},{129,1},{2,130},{3,131},{130,2},{131,3},{4... | collective-permute-start | bytes 811016 | tf_op jit(solution)/shard_map/ppermute | solution.py:62
  116.2 13.6 %collective-permute-start.18 = (bf16[2,528,128]{2,1,0:T(8,128)(2,1)S(1)}, bf16[2,528,128]{2,1,0:T(8,128)(2,1)S(1)}, u32[]{:S(2)}, u32[]{:S(2)}) collective-permute-start(bf16[2,528,128]{2,1,0:T(8,128)(2,1)S(1)} %get-tuple-element.26), channel_id=1, source_target_pairs={{0,129},{1,128},{128,1},{129,0},{2,131},{3,130},{130,3},{131,2},{4... | collective-permute-start | bytes 811016 | tf_op jit(solution)/shard_map/ppermute | solution.py:62
  130.1 11.7 %copy-start = (bf16[1,2048,512]{2,1,0:T(8,128)(2,1)S(1)}, bf16[1,2048,512]{2,1,0:T(8,128)(2,1)}, u32[]{:S(2)}) copy-start(bf16[1,2048,512]{2,1,0:T(8,128)(2,1)} %param.12) | copy-start | bytes 6291460
  130.1 3.9 %collective-permute-start.19 = (bf16[4,528,128]{2,1,0:T(8,128)(2,1)S(1)}, bf16[4,528,128]{2,1,0:T(8,128)(2,1)S(1)}, u32[]{:S(2)}, u32[]{:S(2)}) collective-permute-start(bf16[4,528,128]{2,1,0:T(8,128)(2,1)S(1)} %shard_map.92.own), channel_id=1, source_target_pairs={{0,8},{8,0},{1,9},{9,1},{2,10},{10,2},{3,11},{11,3},{4,12},{12,4},... | collective-permute-start | bytes 1622024 | tf_op jit(solution)/shard_map/ppermute | solution.py:55
  135.8 35.3 %all-to-all-start = ((bf16[8,528,128]{2,1,0:T(8,128)(2,1)}), bf16[8,528,128]{2,1,0:T(8,128)(2,1)S(1)}, u32[]{:S(2)}, u32[]{:S(2)}) async-start(bf16[8,528,128]{2,1,0:T(8,128)(2,1)} %shard_map.93), calls=%async_computation | async-start | bytes 2162688 | tf_op jit(solution)/shard_map/all_to_all | solution.py:360
  141.8 1.0 copy-start.3
  144.4 0.7 copy-start.1
  171.1 1.0 copy-start.2
